TPU v7x, 32 devices: a whole 2x2x4 slice. The times are simulated.
32 devices in a mesh: blk: 8 (over z, core), grp: 4 (over y, x).
Axes of the slice: x: 2, y: 2, z: 4, core: 2. Of those that a mesh axis runs over, the one named last changes fastest.
Arguments:
- signal: bfloat16 [4, 64, 4096], P('grp', None, 'blk'), may hold values from -10 to 10
- lag_table: int32 [512], replicated, may hold values from 0 to 511, each once
- window_end: int32 [4, 8], P('grp', 'blk'), may hold values from 128 to 512
Outputs:
- factors: float32 [4, 512, 512], P('grp', 'blk')
- coeffs: float32 [4, 512, 64], P('grp', 'blk')
- residual: float32 [4, 64, 4096], P('grp', None, 'blk')
Inputs may be any that keep to these rules, and one draw needn't show every extreme that they name: `lag_table`: each of 0 to 511 appears once.
All inputs are finite; a program needn't handle non-finite values.
Results may differ from a plain program's by a relative error of at most 0.0003.
Values may be sent and summed in bfloat16 or wider, within the bound.
A program may use at most 192 MiB of HBM per device.

v0:
```python
import math

import jax
import jax.numpy as jnp
from jax import lax
from jax.sharding import PartitionSpec as P

ridge_weight = 4.0


def passed_along(block, axis, distance):
    devices = range(lax.axis_size(axis))
    route = [((i - distance) % len(devices), i) for i in devices]
    return lax.ppermute(block, axis, route)


def passed_along_2(block, axis, distance):
    devices = range(lax.axis_size(axis))
    route = [(i - distance, i) for i in devices if i - distance in devices]
    return lax.ppermute(block, axis, route)


def entering(x, axis, combine, identity):
    peers, index = (lax.axis_size(axis), lax.axis_index(axis))
    everything = jax.tree.map(lambda part: lax.all_gather(part, axis), x)
    start = jax.tree.map(
        lambda part, zero: jnp.broadcast_to(jnp.asarray(zero, part.dtype), part.shape), x, identity
    )

    def step(k, before):
        reached = k < index
        new = combine(before, jax.tree.map(lambda part: part[k], everything))
        return jax.tree.map(lambda a, b: jnp.where(reached, a, b), new, before)

    return lax.fori_loop(0, peers, step, start)


def lagged_block(history, row_start, block_len, lag_count):
    pieces = [
        lax.dynamic_slice_in_dim(history, row_start + (lag_count - 1 - delay_index), block_len, 1)
        for delay_index in range(lag_count)
    ]
    return jnp.concatenate(pieces, axis=0)


def highest(first_matrix, second_matrix):
    return jnp.dot(first_matrix, second_matrix, precision=lax.Precision.HIGHEST)


def contract_time(first_matrix, second_matrix):
    return lax.dot_general(
        first_matrix, second_matrix, (((1,), (1,)), ((), ())), preferred_element_type=jnp.float32
    )


def upper_of(gram_part):
    return jnp.linalg.cholesky(gram_part).T


def add_pairs(earlier_part, later_part):
    return (earlier_part[0] + later_part[0], earlier_part[1] + later_part[1])


def on_device(signal, lag_table, window_end):
    series = signal[0]
    sensor_count, row_count = series.shape
    col_count = lag_table.shape[0]
    lag_count = col_count // sensor_count
    block_len = min(512, row_count)
    block_count = row_count // block_len
    tail_cols = series[:, row_count - lag_count :]
    prior_cols = passed_along(tail_cols, "blk", 1)
    earlier_cols = passed_along_2(prior_cols, "grp", 1)
    rim_cols = jnp.where(lax.axis_index("blk") == 0, earlier_cols, prior_cols)
    history = jnp.concatenate([rim_cols, series], axis=1)
    end_row = window_end[0, 0]

    def accumulate(step_index, carry_pair):
        gram_part, cross_part = carry_pair
        row_start = step_index * block_len
        lagged = lagged_block(history, row_start, block_len, lag_count)
        target = lax.dynamic_slice_in_dim(history, row_start + lag_count, block_len, 1)
        live_mask = row_start + jnp.arange(block_len, dtype=jnp.int32) < end_row
        masked = jnp.where(live_mask[None, :], lagged, jnp.zeros_like(lagged))
        return (
            gram_part + contract_time(masked, lagged),
            cross_part + contract_time(masked, target),
        )

    start_gram = ridge_weight * jnp.eye(col_count, dtype=jnp.float32)
    start_cross = jnp.zeros((col_count, sensor_count), jnp.float32)
    gram_sum, cross_sum = lax.fori_loop(0, block_count, accumulate, (start_gram, start_cross))
    gram_sum = gram_sum[lag_table][:, lag_table]
    cross_sum = cross_sum[lag_table]
    group_gram, cross_sum = lax.psum((gram_sum, cross_sum), "blk")
    identity = (jnp.zeros_like(group_gram), jnp.zeros_like(cross_sum))
    earlier_part = entering((group_gram, cross_sum), "grp", add_pairs, identity)
    prefix_gram, prefix_cross = add_pairs(earlier_part, (group_gram, cross_sum))
    prefix_factor = upper_of(prefix_gram)
    lower_factor = prefix_factor.T
    half_solved = lax.linalg.triangular_solve(
        lower_factor, prefix_cross, left_side=True, lower=True
    )
    coefficients = lax.linalg.triangular_solve(
        lower_factor, half_solved, left_side=True, lower=True, transpose_a=True
    )
    share_rows = col_count // lax.axis_size("blk")
    first_row = lax.axis_index("blk") * share_rows
    factor_rows = lax.dynamic_slice_in_dim(prefix_factor, first_row, share_rows, 0) / math.sqrt(
        row_count * lax.axis_size("blk")
    )
    coef_rows = lax.dynamic_slice_in_dim(coefficients, first_row, share_rows, 0)
    canonical = jnp.zeros_like(coefficients).at[lag_table].set(coefficients)

    def residual_step(step_index, output):
        row_start = step_index * block_len
        lagged = lagged_block(history, row_start, block_len, lag_count).astype(jnp.float32)
        target = lax.dynamic_slice_in_dim(history, row_start + lag_count, block_len, 1).astype(
            jnp.float32
        )
        fitted = highest(canonical.T, lagged)
        return lax.dynamic_update_slice_in_dim(output, target - fitted, row_start, 1)

    residual = lax.fori_loop(
        0, block_count, residual_step, jnp.zeros((sensor_count, row_count), jnp.float32)
    )
    return (factor_rows[None], coef_rows[None], residual[None])


def solution(mesh):
    return jax.shard_map(
        on_device,
        mesh=mesh,
        in_specs=(P("grp", None, "blk"), P(), P("grp", "blk")),
        out_specs=(P("grp", "blk", None), P("grp", "blk", None), P("grp", None, "blk")),
        check_vma=False,
    )
```

profile of v0, /device:TPU:5, one launch (start us, length us, event | category | flops | bytes accessed | tf_op | source)
XLA Modules:
  0.0 311.9 jit_solution(4231370352947032965)
XLA Ops:
  8.0 1.9 collective-permute-start
  11.2 3.1 %collective-permute-start.1 = (bf16[64,8]{1,0:T(8,128)(2,1)S(1)}, bf16[64,8]{1,0:T(8,128)(2,1)S(1)}, u32[]{:S(2)}, u32[]{:S(2)}) collective-permute-start(bf16[64,8]{1,0:T(8,128)(2,1)S(1)} %collective-permute-done), channel_id=1, source_target_pairs={{0,1},{1,2},{2,3},{4,5},{5,6},{6,7},{8,9},{9,10},{10,11},{12,13},{... | collective-permute-start | bytes 3080 | tf_op jit(solution)/shard_map/ppermute | solution.py:20
  14.4 2.2 collective-permute-done.1
  24.9 1.1 fusion.3
  26.0 1.6 gather_fusion
  28.0 2.3 gather_fusion.1
  30.3 1.6 gather_fusion.2
  32.0 60.1 %all-reduce.4.cloned.1.call-done = (f32[512,512]{0,1:T(8,128)}, f32[512,64]{1,0:T(8,128)}) async-done(((f32[512,512]{0,1:T(8,128)}, f32[512,64]{1,0:T(8,128)}), (f32[512,512]{0,1:T(8,128)}, f32[512,64]{1,0:T(8,128)})) %all-reduce.4.cloned.1.call-update) | async-done | bytes 1179664 | tf_op jit(solution)/shard_map/psum | solution.py:95
  92.2 11.1 %all-gather.1 = f32[2048,64]{1,0:T(8,128)S(1)} all-gather(f32[512,64]{1,0:T(8,128)} %get-tuple-element.216), channel_id=3, replica_groups=mesh['blk'=8,'grp'=4] {'grp'}, dimensions={0}, use_global_device_ids=true | all-gather | bytes 655360 | tf_op jit(solution)/shard_map/all_gather | solution.py:25
  103.3 44.1 %all-gather.4.cloned.1.call-done = f32[2048,512]{0,1:T(8,128)} async-done(((f32[512,512]{0,1:T(8,128)}), f32[2048,512]{0,1:T(8,128)}) %all-gather.4.cloned.1.call-update) | async-done | bytes 4194320 | tf_op jit(solution)/shard_map/all_gather | solution.py:25
  147.4 5.3 %copy.29 = f32[2048,512]{1,0:T(8,128)} copy(f32[2048,512]{0,1:T(8,128)} %all-gather.4.cloned.1.call-done) | data formatting | bytes 8388608
  152.8 7.0 %while.12 = (s32[]{:T(128)}, f32[512,512]{1,0:T(8,128)S(1)}, f32[512,64]{1,0:T(8,128)S(1)}, s32[]{:T(128)}, f32[4,512,512]{2,1,0:T(8,128)}, /*index=5*/f32[4,512,64]{2,1,0:T(8,128)S(1)}, s32[]{:T(128)}, s32[]{:T(128)}) while((s32[]{:T(128)}, f32[512,512]{1,0:T(8,128)S(1)}, f32[512,64]{1,0:T(8,128)S(1)}, s32[]{:T(128)}, ...), condition=%wide.region_3.4_spmd.clone, body=%wide.region_2.3_spmd.clone.sunk | while | flops 884740 | bytes 3539059 | solution.py:35
  152.8 1.7 add_select_fusion.4
  154.6 1.6 add_select_fusion.4
  156.2 1.6 add_select_fusion.4
  157.9 1.6 add_select_fusion.4
  161.0 11.7 %cholesky.103 = f32[128,128]{1,0:T(8,128)S(1)} custom-call(f32[128,128]{1,0:T(8,128)S(1)} %cholesky.263), custom_call_target="Cholesky" | custom-call | tf_op jit(solution)/shard_map/jit(cholesky)/cholesky | solution.py:57
  172.7 9.8 %custom-call.32 = f32[1,128,128]{1,2,0:T(8,128)S(1)} custom-call(f32[1,128,128]{2,1,0:T(8,128)S(1)} %get-tuple-element.230), custom_call_target="InvertDiagBlocksLowerTriangular" | custom-call | tf_op jit(solution)/shard_map/jit(cholesky)/cholesky | solution.py:57
  183.7 11.7 %cholesky.215 = f32[128,128]{1,0:T(8,128)S(1)} custom-call(f32[128,128]{1,0:T(8,128)S(1)} %cholesky.267), custom_call_target="Cholesky" | custom-call | tf_op jit(solution)/shard_map/jit(cholesky)/cholesky | solution.py:57
  195.5 10.0 %custom-call.33 = f32[1,128,128]{1,2,0:T(8,128)S(1)} custom-call(f32[1,128,128]{2,1,0:T(8,128)S(1)} %get-tuple-element.227), custom_call_target="InvertDiagBlocksLowerTriangular" | custom-call | tf_op jit(solution)/shard_map/jit(cholesky)/cholesky | solution.py:57
  206.2 11.7 %cholesky.236 = f32[128,128]{1,0:T(8,128)S(1)} custom-call(f32[128,128]{1,0:T(8,128)S(1)} %cholesky.272), custom_call_target="Cholesky" | custom-call | tf_op jit(solution)/shard_map/jit(cholesky)/cholesky | solution.py:57
  218.6 9.8 %custom-call.34 = f32[1,128,128]{1,2,0:T(8,128)S(1)} custom-call(f32[1,128,128]{2,1,0:T(8,128)S(1)} %get-tuple-element.224), custom_call_target="InvertDiagBlocksLowerTriangular" | custom-call | tf_op jit(solution)/shard_map/jit(cholesky)/cholesky | solution.py:57
  229.0 11.9 %cholesky.253 = f32[128,128]{1,0:T(8,128)S(1)} custom-call(f32[128,128]{1,0:T(8,128)S(1)} %convolution_subtract_fusion.6), custom_call_target="Cholesky" | custom-call | tf_op jit(solution)/shard_map/jit(cholesky)/cholesky | solution.py:57
  245.1 10.4 %while.11 = (s32[]{:T(128)}, f32[512,512]{1,0:T(8,128)S(1)}, s32[4,2]{0,1:T(2,128)S(1)}, f32[4,128,128]{2,1,0:T(8,128)}, s32[]{:T(128)}) while((s32[]{:T(128)}, f32[512,512]{1,0:T(8,128)S(1)}, s32[4,2]{0,1:T(2,128)S(1)}, f32[4,128,128]{2,1,0:T(8,128)}, s32[]{:T(128)}) %tuple.69), condition=%wide.while_cond, body=%wide.while_body.sunk | while | flops 2 | bytes 132705 | solution.py:104
  245.8 2.0 bitcast_dynamic-update-slice_fusion.2
  248.4 2.0 bitcast_dynamic-update-slice_fusion.2
  251.0 2.0 bitcast_dynamic-update-slice_fusion.2
  253.6 2.0 bitcast_dynamic-update-slice_fusion.2
  255.6 40.1 %custom-call.35 = f32[4,128,128]{1,2,0:T(8,128)S(1)} custom-call(f32[4,128,128]{2,1,0:T(8,128)} %get-tuple-element.155), custom_call_target="InvertDiagBlocksLowerTriangular" | custom-call | tf_op jit(solution)/shard_map/triangular_solve | solution.py:104
  295.7 1.0 add.191
  300.5 1.8 scatter_custom_fusion
  302.3 1.1 fusion
  (89 shorter events, 24.1 us)
Async XLA Ops:
  7.2 85.0 %all-reduce.4.cloned.1.call-start = ((), (), s32[]{:S(2)}) async-start(), calls=%async_computation.1 | async-start | bytes 2621440 | tf_op jit(solution)/shard_map/psum | solution.py:95
  8.0 3.2 %collective-permute-start = (bf16[64,8]{1,0:T(8,128)(2,1)S(1)}, bf16[64,8]{1,0:T(8,128)(2,1)S(1)}, u32[]{:S(2)}, u32[]{:S(2)}) collective-permute-start(bf16[64,8]{1,0:T(8,128)(2,1)S(1)} %slice.155), channel_id=1, source_target_pairs={{28,0},{0,4},{4,8},{8,12},{12,16},{16,20},{20,24},{24,28},{29,1},{... | collective-permute-start | bytes 3080 | tf_op jit(solution)/shard_map/ppermute | solution.py:14
  11.2 5.4 %collective-permute-start.1 = (bf16[64,8]{1,0:T(8,128)(2,1)S(1)}, bf16[64,8]{1,0:T(8,128)(2,1)S(1)}, u32[]{:S(2)}, u32[]{:S(2)}) collective-permute-start(bf16[64,8]{1,0:T(8,128)(2,1)S(1)} %collective-permute-done), channel_id=1, source_target_pairs={{0,1},{1,2},{2,3},{4,5},{5,6},{6,7},{8,9},{9,10},{10,11},{12,13},{... | collective-permute-start | bytes 3080 | tf_op jit(solution)/shard_map/ppermute | solution.py:20
  24.1 0.8 copy-start.2
  32.0 115.4 %all-gather.4.cloned.1.call-start = ((), (), s32[]{:S(2)}) async-start(), calls=%async_computation | async-start | bytes 5242880 | tf_op jit(solution)/shard_map/all_gather | solution.py:25
  152.8 7.4 %copy-start.1 = (f32[512,512]{0,1:T(8,128)S(1)}, f32[512,512]{0,1:T(8,128)}, u32[]{:S(2)}) copy-start(f32[512,512]{0,1:T(8,128)} %get-tuple-element.215) | copy-start | bytes 3145732
  244.8 57.4 %copy-start = (bf16[1,64,512]{2,1,0:T(8,128)(2,1)S(1)}, bf16[1,64,512]{2,1,0:T(8,128)(2,1)}, u32[]{:S(2)}) copy-start(bf16[1,64,512]{2,1,0:T(8,128)(2,1)} %param.5) | copy-start | bytes 196612
  245.1 57.1 %copy-start.3 = (bf16[512,512]{1,0:T(8,128)(2,1)S(1)}, bf16[512,512]{1,0:T(8,128)(2,1)}, u32[]{:S(2)}) copy-start(bf16[512,512]{1,0:T(8,128)(2,1)} %copy-done.2) | copy-start | bytes 1572868
Sparse Core Ops, SparseCore 0:
  32.1 59.9 all-reduce.3
  94.0 53.4 all-gather.3
where the time goes:
time: 314 us; the launch traced here: 312 us
  other arithmetic  136 us (43%)
  waiting for transfers between devices  107 us (34%)
  local copies, waits for them, and re-layouts  27.2 us (9%)
  between operations  17.7 us (6%)
  blocking collectives  11.1 us (4%)
  matrix products  8.31 us (3%)
  starting transfers between devices  5.06 us (2%)
    another operation x14, other arithmetic, upper_of(): return jnp.linalg.cholesky(gram_part).T  78.8 us
    psum x1, waiting for transfers between devices, on_device(): group_gram, cross_sum = lax.psum((gram_sum, cross_sum), 'blk')  60.1 us
    all_gather x1, waiting for transfers between devices, entering(): everything = jax.tree.map(lambda part: lax.all_gather(part, axis), x)  44.1 us
    another operation x4, other arithmetic, on_device(): lax.linalg.triangular_solve(lower_factor, half_solved, left_side=True, lo...  40.4 us
    all_gather x1, blocking collectives, entering(): everything = jax.tree.map(lambda part: lax.all_gather(part, axis), x)  11.1 us
    another operation x12, local copies, waits for them, and re-layouts  10.4 us
    select_n x8, other arithmetic, step(): return jax.tree.map(lambda a, b: jnp.where(reached, a, b), new, before)  6.75 us
    unnamed x10, other arithmetic  6.52 us
  transfers between devices with their start and end apart: 4, of which 3 were waited for; matrix products, arithmetic and copies ran while one was open for 0% of the time, Pallas kernels for 0%

commit v1 on v0

v1 whole, which is shorter than its diff:
```python
import functools
import math

import jax
import jax.numpy as jnp
from jax import lax
from jax.experimental import pallas as pl
from jax.experimental.pallas import tpu as pltpu
from jax.sharding import PartitionSpec as P

ridge_weight = 4.0
LAGS = 8
TILE = 128
WIDE = 640
MESH = pl.DeviceIdType.MESH
VMEM = pltpu.VMEM
F32 = jnp.float32
BF16 = jnp.bfloat16


def iota(shape, dim):
    return lax.broadcasted_iota(jnp.int32, shape, dim)


def dot(a, b):
    return jnp.dot(a, b, preferred_element_type=F32)


def dot_nt(a, b):
    return lax.dot_general(a, b, (((1,), (1,)), ((), ())), preferred_element_type=F32)


def exact_dot(a, b):
    return jnp.dot(a, b, precision=lax.Precision.HIGHEST, preferred_element_type=F32)


def split3(x):
    hi = x.astype(BF16)
    rest = x - hi.astype(F32)
    mid = rest.astype(BF16)
    low = (rest - mid.astype(F32)).astype(BF16)
    return hi, mid, low


def delayed(x, delay):
    if delay == 0:
        return x
    return jnp.where(iota(x.shape, 1) < delay, 0.0, pltpu.roll(x, delay, 1))


def moments_kernel(end_ref, x_ref, c_ref, e_ref):
    x = x_ref[0].astype(F32)
    sensors, rows = x.shape
    end = end_ref[0, 0]
    stack = [delayed(x, d) for d in range(LAGS + 1)] + [jnp.zeros_like(x)]
    z = jnp.concatenate(stack, axis=0).astype(BF16)
    xm = jnp.where(iota(x.shape, 1) < end, x, 0.0).astype(BF16)
    c_ref[...] = dot_nt(xm, z).reshape(c_ref.shape)
    row, time = iota((16, rows), 0), iota((16, rows), 1)
    head_tail = jnp.where(row < 8, row, rows - 16 + row)
    last_live = jnp.where(row < 8, -1, end - 16 + row)
    sel_a = jnp.where(time == head_tail, 1.0, 0.0).astype(BF16)
    sel_b = jnp.where(time == last_live, 1.0, 0.0).astype(BF16)
    xl = jnp.concatenate([x, jnp.zeros_like(x)], axis=0).astype(BF16)
    xr = jnp.concatenate([jnp.zeros_like(x), x], axis=0).astype(BF16)
    e_ref[...] = (dot_nt(sel_a, xl) + dot_nt(sel_b, xr)).astype(BF16)


def share_kernel(nblk, ngrp, ns, c_ref, e_ref, sum_ref, edge_ref,
                 part, group_edge, prior, all_edge, mine, whole,
                 send1, recv1, send1e, recv1e, send2, recv2, send2e, recv2e, send3, recv3):
    b, g = lax.axis_index("blk"), lax.axis_index("grp")
    owner = (lambda i: True) if ns == nblk else (lambda i: i < ns)

    def when(cond, fn):
        if cond is True:
            fn()
        else:
            pl.when(cond)(fn)

    prior[...] = jnp.zeros_like(prior)
    all_edge[...] = jnp.zeros_like(all_edge)
    barrier = pltpu.get_barrier_semaphore()
    for off in range(1, nblk):
        pl.semaphore_signal(barrier, inc=1, device_id=(lax.rem(b + off, nblk), g), device_id_type=MESH)
    for off in range(1, ngrp):
        pl.semaphore_signal(barrier, inc=1, device_id=(b, lax.rem(g + off, ngrp)), device_id_type=MESH)
    pl.semaphore_wait(barrier, nblk - 1 + ngrp - 1)

    def slice_copy(to, frm, off):
        return pltpu.make_async_remote_copy(
            src_ref=c_ref.at[to], dst_ref=part.at[frm], send_sem=send1.at[off], recv_sem=recv1.at[frm],
            device_id=(to, g), device_id_type=MESH)

    def edge_copy(to, frm, off):
        return pltpu.make_async_remote_copy(
            src_ref=e_ref, dst_ref=group_edge.at[frm], send_sem=send1e.at[off], recv_sem=recv1e.at[frm],
            device_id=(to, g), device_id_type=MESH)

    for off in range(1, nblk):
        to = lax.rem(b + off, nblk)
        when(owner(to), lambda: slice_copy(to, b, off).start())
        edge_copy(to, b, off).start()
    when(owner(b), lambda: part.__setitem__(b, c_ref[b]))
    group_edge[b] = e_ref[...]
    for off in range(1, nblk):
        frm = lax.rem(b + nblk - off, nblk)
        when(owner(b), lambda: slice_copy(b, frm, off).wait_recv())
        edge_copy(b, frm, off).wait_recv()

    def total():
        acc = part[0]
        for i in range(1, nblk):
            acc = acc + part[i]
        mine[...] = acc

    when(owner(b), total)
    all_edge[g] = group_edge[...]

    def sum_copy(to, frm):
        return pltpu.make_async_remote_copy(
            src_ref=mine, dst_ref=prior.at[frm], send_sem=send2.at[to], recv_sem=recv2.at[frm],
            device_id=(b, to), device_id_type=MESH)

    def edges_copy(to, frm):
        return pltpu.make_async_remote_copy(
            src_ref=group_edge, dst_ref=all_edge.at[frm], send_sem=send2e.at[to], recv_sem=recv2e.at[frm],
            device_id=(b, to), device_id_type=MESH)

    for h in range(1, ngrp):
        @pl.when(h > g)
        def _():
            when(owner(b), lambda: sum_copy(h, g).start())
            edges_copy(h, g).start()
    for h in range(ngrp - 1):
        @pl.when(h < g)
        def _():
            when(owner(b), lambda: sum_copy(g, h).wait_recv())

    def prefix():
        acc = mine[...]
        for h in range(ngrp - 1):
            acc = acc + prior[h]
        whole[b] = acc

    when(owner(b), prefix)

    def whole_copy(to, frm, off):
        return pltpu.make_async_remote_copy(
            src_ref=whole.at[frm], dst_ref=whole.at[frm], send_sem=send3.at[off], recv_sem=recv3.at[frm],
            device_id=(to, g), device_id_type=MESH)

    for off in range(1, nblk):
        when(owner(b), lambda: whole_copy(lax.rem(b + off, nblk), b, off).start())
    for h in range(ngrp - 1):
        @pl.when(h < g)
        def _():
            edges_copy(g, h).wait_recv()
    edge_ref[...] = all_edge[...]
    for off in range(1, nblk):
        frm = lax.rem(b + nblk - off, nblk)
        when(owner(frm), lambda: whole_copy(b, frm, off).wait_recv())
    sum_ref[...] = whole[...]
    for off in range(1, nblk):
        to = lax.rem(b + off, nblk)
        when(owner(to), lambda: slice_copy(to, b, off).wait_send())
        edge_copy(to, b, off).wait_send()
        when(owner(b), lambda: whole_copy(to, b, off).wait_send())
    for h in range(1, ngrp):
        @pl.when(h > g)
        def _():
            when(owner(b), lambda: sum_copy(h, g).wait_send())
            edges_copy(h, g).wait_send()


def lower_inverse(block, out_ref, r0):
    n = TILE // 8
    lane, sub = iota((8, TILE), 1), iota((8, TILE), 0)
    x = [block[8 * r : 8 * r + 8, :] for r in range(n)]

    def rep_lane(v, j):
        return jnp.broadcast_to(v[:, j : j + 1], (8, TILE))

    def rep_row(v, i):
        return jnp.broadcast_to(v[i : i + 1, :], (8, TILE))

    for q in range(n):
        first = 8 * q
        cols = [rep_lane(x[q], first + j) for j in range(8)]
        t = {(i, j): rep_row(cols[j], i) for j in range(8) for i in range(j, 8)}
        inside = (lane >= first) & (lane < first + 8)
        aug = jnp.where(inside, jnp.where(lane - first == sub, 1.0, 0.0), x[q])
        y = [rep_row(aug, i) for i in range(8)]
        inv, l, scaled = [], {}, []
        for j in range(8):
            p = t[j, j]
            inv.append(1.0 / p)
            scaled.append(y[j] * lax.rsqrt(p))
            for i in range(j + 1, 8):
                l[i, j] = t[i, j] * inv[j]
            for k in range(j + 1, 8):
                for i in range(k, 8):
                    t[i, k] = t[i, k] - l[i, j] * t[k, j]
            for i in range(j + 1, 8):
                y[i] = y[i] - l[i, j] * y[j]
        rows = scaled[0]
        for i in range(1, 8):
            rows = jnp.where(sub == i, scaled[i], rows)
        out_ref[pl.ds(pl.multiple_of(r0 + first, 8), 8), :] = jnp.where(lane < first + 8, rows, 0.0)
        if q == n - 1:
            break
        gs = [None] * 8
        for i in range(7, -1, -1):
            acc = y[i] * inv[i]
            for k in range(7, i, -1):
                acc = acc - l[k, i] * gs[k]
            gs[i] = acc
        for r in range(q + 1, n):
            new = jnp.where(inside, 0.0, x[r])
            for j in range(7, -1, -1):
                new = new - rep_lane(x[r], first + j) * gs[j]
            x[r] = new


def fit_kernel(nblk, ngrp, x_ref, lagc_ref, lagr_ref, c_ref, e_ref, fac_ref, coef_ref, res_ref,
               a, ps, pe, tl, vt, dm, miss, u, li, w):
    b, g = lax.axis_index("blk"), lax.axis_index("grp")
    cols = a.shape[0]
    x = x_ref[0].astype(F32)
    sensors, rows = x.shape
    half = nblk * 8

    ps[...] = jnp.zeros_like(ps)
    pe[...] = jnp.zeros_like(pe)
    tl[...] = jnp.zeros_like(tl)
    dm[...] = jnp.zeros_like(dm)
    miss[...] = jnp.zeros_like(miss)
    lane3 = iota((nblk, 16, TILE), 2)
    left = iota((nblk, 8, TILE), 2) < sensors

    def group_edges(h, carry):
        e = e_ref[h].astype(F32)
        turned = pltpu.roll(e.reshape(nblk * 16, TILE), sensors, 1).reshape(nblk, 16, TILE)
        lo = jnp.where(lane3 < sensors, e, turned)
        hi = jnp.where(lane3 < sensors, turned, e)
        ps[0, 0:8, :] = tl[...]
        if nblk > 1:
            ps[1:, 0:8, :] = lo[: nblk - 1, 8:16, :]
        tl[...] = lo[nblk - 1, 8:16, :]
        pe[:, 0:8, :] = hi[:, 8:16, :]
        head = lo[:, 0:8, :].reshape(half, TILE)
        for i in range(LAGS // 2):
            even, odd = 2 * i + 1, 2 * i + 2
            for ref, at in ((ps, 0), (pe, half)):
                part = jnp.where(left, ref[:, pl.ds(8 - even, 8), :], ref[:, pl.ds(8 - odd, 8), :])
                vt[at : at + half, i * TILE : (i + 1) * TILE] = part.reshape(half, TILE)
        v = vt[...]
        signed = jnp.where(iota(v.shape, 0) < half, v, -v)
        v16 = v.astype(BF16)
        dm[...] += dot(signed.T.astype(BF16), v16)
        miss[...] += dot(head.T.astype(BF16), v16[:half])
        return carry

    lax.fori_loop(0, g + 1, group_edges, 0)

    more = jnp.concatenate([miss[0:sensors, :], jnp.zeros((sensors, TILE), F32)], axis=1)
    c = c_ref[...].reshape(sensors, WIDE) + pltpu.roll(more, sensors, 1)
    cm = jnp.where(iota(c.shape, 1) < sensors, 0.5 * c, c)
    cr = pltpu.roll(cm, sensors, 1)
    a[...] = jnp.zeros_like(a)
    for i in range(LAGS):
        base = sensors * (i - i % 2)
        a[sensors * i : sensors * (i + 1), base:cols] = (cr if i % 2 else cm)[:, : cols - base]
    gu = a[:, :cols]
    ridge = (ridge_weight * nblk) * (g + 1).astype(F32)
    eye = jnp.where(iota((cols, cols), 0) == iota((cols, cols), 1), ridge, 0.0)
    gram = gu + gu.T + dm[...] + eye
    cross = jnp.concatenate([c, jnp.zeros_like(c)], axis=0).T[sensors : sensors + cols, :]
    both = jnp.concatenate([gram, cross], axis=1)
    pick = jnp.where(lagc_ref[...] == iota((cols, cols), 1), 1.0, 0.0).astype(BF16)
    pick_t = jnp.where(lagr_ref[...] == iota((cols, cols), 0), 1.0, 0.0).astype(BF16)
    hi, mid, low = split3(both)
    turned = dot(pick, hi) + dot(pick, mid) + dot(pick, low)
    a[:, cols:] = turned[:, cols:]
    hi, mid, low = split3(turned[:, :cols])
    a[:, :cols] = dot(hi, pick_t) + dot(mid, pick_t) + dot(low, pick_t)

    steps = cols // TILE

    def eliminate(k, carry):
        r0 = pl.multiple_of(k * TILE, TILE)
        lower_inverse(a[pl.ds(r0, TILE), pl.ds(r0, TILE)], li, r0)
        panel = exact_dot(li[pl.ds(r0, TILE), :], a[pl.ds(r0, TILE), :])
        panel = jnp.where(iota(panel.shape, 1) >= iota(panel.shape, 0) + r0, panel, 0.0)
        u[pl.ds(r0, TILE), :] = panel

        @pl.when(k < steps - 1)
        def _():
            a[...] -= exact_dot(panel[:, :cols].T, panel)

        return carry

    lax.fori_loop(0, steps, eliminate, 0)

    w[...] = jnp.zeros_like(w)
    for k in range(steps - 1, -1, -1):
        at = slice(k * TILE, (k + 1) * TILE)
        rhs = u[at, cols:]
        if k < steps - 1:
            rhs = rhs - exact_dot(u[at, (k + 1) * TILE : cols], w[(k + 1) * TILE :, :])
        w[at, :] = exact_dot(li[at, :].T, rhs)

    share = cols // nblk
    row0 = pl.multiple_of(b * share, share)
    fac_ref[0] = u[pl.ds(row0, share), :cols] * (1.0 / math.sqrt(rows * nblk))
    coef_ref[0] = w[pl.ds(row0, share), :][:, :sensors]

    hi, mid, low = split3(w[...])
    canon = (dot(pick_t, hi) + dot(pick_t, mid) + dot(pick_t, low)).T[:sensors, :]
    hi, mid, low = split3(canon)
    z = jnp.concatenate([delayed(x, d) for d in range(1, LAGS + 1)], axis=0).astype(BF16)
    fitted = dot(hi, z) + dot(mid, z) + dot(low, z)
    own = vt[pl.ds(pl.multiple_of(b * 8, 8), 8), :]
    own = jnp.concatenate([own, jnp.zeros((TILE - 8, cols), F32)], axis=0).astype(BF16)
    rim = dot_nt(hi, own) + dot_nt(mid, own) + dot_nt(low, own)
    res = x - fitted
    res_ref[0, :, :TILE] = res[:, :TILE] - rim
    res_ref[0, :, TILE:] = res[:, TILE:]


def on_device(nblk, ngrp, signal, lag_table, window_end):
    _, sensors, rows = signal.shape
    cols = lag_table.shape[0]
    ns = min(nblk, sensors // 8)
    per = sensors // ns
    vmem = pl.BlockSpec(memory_space=VMEM)
    smem = pl.BlockSpec(memory_space=pltpu.SMEM)
    dma = pltpu.SemaphoreType.DMA
    c, e = pl.pallas_call(
        moments_kernel,
        out_shape=(jax.ShapeDtypeStruct((ns, per, WIDE), F32), jax.ShapeDtypeStruct((16, TILE), BF16)),
        in_specs=[smem, vmem],
        out_specs=(vmem, vmem),
    )(window_end, signal)
    sums, edges = pl.pallas_call(
        functools.partial(share_kernel, nblk, ngrp, ns),
        out_shape=(jax.ShapeDtypeStruct((ns, per, WIDE), F32),
                   jax.ShapeDtypeStruct((ngrp, nblk, 16, TILE), BF16)),
        in_specs=[vmem, vmem],
        out_specs=(vmem, vmem),
        scratch_shapes=[
            VMEM((nblk, per, WIDE), F32), VMEM((nblk, 16, TILE), BF16),
            VMEM((ngrp, per, WIDE), F32), VMEM((ngrp, nblk, 16, TILE), BF16),
            VMEM((per, WIDE), F32), VMEM((ns, per, WIDE), F32),
            dma((nblk,)), dma((nblk,)), dma((nblk,)), dma((nblk,)),
            dma((ngrp,)), dma((ngrp,)), dma((ngrp,)), dma((ngrp,)),
            dma((nblk,)), dma((nblk,)),
        ],
        compiler_params=pltpu.CompilerParams(
            collective_id=0, has_side_effects=True, vmem_limit_bytes=32 * 1024 * 1024),
    )(c, e)
    half = nblk * 8
    share = cols // nblk
    return pl.pallas_call(
        functools.partial(fit_kernel, nblk, ngrp),
        out_shape=(jax.ShapeDtypeStruct((1, share, cols), F32),
                   jax.ShapeDtypeStruct((1, share, sensors), F32),
                   jax.ShapeDtypeStruct((1, sensors, rows), F32)),
        in_specs=[vmem] * 5,
        out_specs=(vmem, vmem, vmem),
        scratch_shapes=[
            VMEM((cols, WIDE), F32), VMEM((nblk, 16, TILE), F32), VMEM((nblk, 16, TILE), F32),
            VMEM((8, TILE), F32), VMEM((2 * half, cols), F32), VMEM((cols, cols), F32),
            VMEM((TILE, cols), F32), VMEM((cols, WIDE), F32), VMEM((cols, TILE), F32),
            VMEM((cols, TILE), F32),
        ],
        compiler_params=pltpu.CompilerParams(vmem_limit_bytes=48 * 1024 * 1024),
    )(signal, lag_table.reshape(cols, 1), lag_table.reshape(1, cols), sums, edges)


def solution(mesh):
    return jax.shard_map(
        functools.partial(on_device, mesh.shape["blk"], mesh.shape["grp"]),
        mesh=mesh,
        in_specs=(P("grp", None, "blk"), P(), P("grp", "blk")),
        out_specs=(P("grp", "blk", None), P("grp", "blk", None), P("grp", None, "blk")),
        check_vma=False,
    )
```

time: 314 us -> 58.4 us (0.19)
  other arithmetic: 136 us -> 0 us
  waiting for transfers between devices: 107 us -> 0 us
  Pallas kernels: 0 us -> 53.1 us
  local copies, waits for them, and re-layouts: 27.2 us -> 3.11 us
  between operations: 17.7 us -> 1.3 us
  blocking collectives: 11.1 us -> 0 us
  matrix products: 8.31 us -> 0 us
  starting transfers between devices: 5.06 us -> 0 us
    another operation x18 -> x0, other arithmetic: 119 us -> none  [the longest x14 78.8 us: upper_of(): return jnp.linalg.cholesky(gram_part).T]
    psum x1 -> x0, waiting for transfers between devices: 60.1 us -> none  [on_device(): group_gram, cross_sum = lax.psum((gram_sum, cross_sum), 'blk')]
    pallas_call x0 -> x3, Pallas kernels: none -> 53.1 us  [the longest x1 33.7 us: on_device(): pl.pallas_call(functools.partial(fit_kernel, nblk, ngrp), out_shape=(jax....]
    all_gather x1 -> x0, waiting for transfers between devices: 44.1 us -> none  [entering(): everything = jax.tree.map(lambda part: lax.all_gather(part, axis), x)]
    all_gather x1 -> x0, blocking collectives: 11.1 us -> none  [entering(): everything = jax.tree.map(lambda part: lax.all_gather(part, axis), x)]
    another operation x20 -> x0, local copies, waits for them, and re-layouts: 10.8 us -> none
    select_n x10 -> x0, other arithmetic: 7.44 us -> none  [the longest x8 6.75 us: step(): return jax.tree.map(lambda a, b: jnp.where(reached, a, b), new, before)]
    unnamed x10 -> x0, other arithmetic: 6.52 us -> none
  transfers between devices with their start and end apart: 4 -> 0, of which waited for: 3 -> 0; matrix products, arithmetic and copies ran while one was open for 0% -> 0% of each run, Pallas kernels for 0% -> 0%
where the time goes in v1:
time: 58.4 us; the launch traced here: 57.5 us
  Pallas kernels  53.1 us (91%)
  local copies, waits for them, and re-layouts  3.11 us (5%)
  between operations  1.3 us (2%)
    pallas_call x1, Pallas kernels, on_device(): pl.pallas_call(functools.partial(fit_kernel, nblk, ngrp), out_shape=(jax....  33.7 us
    pallas_call x1, Pallas kernels, on_device(): pl.pallas_call(functools.partial(share_kernel, nblk, ngrp, ns), out_shape...  17.5 us
    unnamed x8, local copies, waits for them, and re-layouts  2.97 us
    pallas_call x1, Pallas kernels, on_device(): pl.pallas_call(moments_kernel, out_shape=(jax.ShapeDtypeStruct((ns, per,...  1.92 us

profile of v1, /device:TPU:5, one launch (start us, length us, event | category | flops | bytes accessed | tf_op | source)
XLA Modules:
  0.0 57.5 jit_solution(18353831742961325403)
XLA Ops:
  1.3 1.9 %shard_map.58 = (f32[8,8,640]{2,1,0:T(8,128)}, bf16[16,128]{1,0:T(8,128)(2,1)}) custom-call(s32[1,1]{1,0:T(1,128)S(6)} %copy.7.end_ref, bf16[1,64,512]{2,1,0:T(8,128)(2,1)} %x_ref.3), custom_call_target="tpu_custom_call" | custom-call | tf_op jit(solution)/shard_map/pallas_call | solution.py:339
  3.2 0.0 copy-start.1
  3.2 0.9 %copy-done.1 = f32[8,8,640]{2,1,0:T(8,128)S(1)} copy-done((f32[8,8,640]{2,1,0:T(8,128)S(1)}, f32[8,8,640]{2,1,0:T(8,128)}, u32[]{:S(2)}) %copy-start.1) | copy-done | bytes 163864
  4.1 0.0 copy-start.3
  4.1 0.7 %copy-done.3 = bf16[16,128]{1,0:T(8,128)(2,1)S(1)} copy-done((bf16[16,128]{1,0:T(8,128)(2,1)S(1)}, bf16[16,128]{1,0:T(8,128)(2,1)}, u32[]{:S(2)}) %copy-start.3) | copy-done | bytes 4120
  4.8 17.5 %shard_map.59 = (f32[8,8,640]{2,1,0:T(8,128)S(1)}, bf16[4,8,16,128]{3,2,1,0:T(8,128)(2,1)S(1)}) custom-call(f32[8,8,640]{2,1,0:T(8,128)S(1)} %copy-done.1, bf16[16,128]{1,0:T(8,128)(2,1)S(1)} %copy-done.3), custom_call_target="tpu_custom_call" | custom-call | tf_op jit(solution)/shard_map/pallas_call | solution.py:345
  22.3 0.0 copy-start.2
  22.3 0.7 %copy-done.2 = s32[512]{0:T(512)S(1)} copy-done((s32[512]{0:T(512)S(1)}, s32[512]{0:T(512)}, u32[]{:S(2)}) %copy-start.2) | copy-done | bytes 2072
  23.0 0.0 copy-start
  23.0 0.1 copy.6.lagc_ref
  23.1 0.7 %copy-done = bf16[1,64,512]{2,1,0:T(8,128)(2,1)S(1)} copy-done((bf16[1,64,512]{2,1,0:T(8,128)(2,1)S(1)}, bf16[1,64,512]{2,1,0:T(8,128)(2,1)}, u32[]{:S(2)}) %copy-start) | copy-done | bytes 65560
  23.8 33.7 %shard_map.60 = (f32[1,64,512]{2,1,0:T(8,128)}, f32[1,64,64]{2,1,0:T(8,128)}, f32[1,64,512]{2,1,0:T(8,128)}) custom-call(bf16[1,64,512]{2,1,0:T(8,128)(2,1)S(1)} %copy-done, s32[512,1]{1,0:T(8,128)S(1)} %copy.6.lagc_ref, s32[1,512]{1,0:T(1,128)S(1)} %bitcast.3, f32[8,8,640]{2,1,0:T(8,128)S(1)} %get-tuple-element.9.c_ref, ...), custom_call_target="tpu_custom_call" | custom-call | tf_op jit(solution)/shard_map/pallas_call | solution.py:364
Async XLA Ops:
  3.2 0.9 %copy-start.1 = (f32[8,8,640]{2,1,0:T(8,128)S(1)}, f32[8,8,640]{2,1,0:T(8,128)}, u32[]{:S(2)}) copy-start(f32[8,8,640]{2,1,0:T(8,128)} %get-tuple-element.7.c_ref) | copy-start | bytes 491524
  4.1 0.7 %copy-start.3 = (bf16[16,128]{1,0:T(8,128)(2,1)S(1)}, bf16[16,128]{1,0:T(8,128)(2,1)}, u32[]{:S(2)}) copy-start(bf16[16,128]{1,0:T(8,128)(2,1)} %get-tuple-element.8.e_ref) | copy-start | bytes 12292
  22.3 0.7 %copy-start.2 = (s32[512]{0:T(512)S(1)}, s32[512]{0:T(512)}, u32[]{:S(2)}) copy-start(s32[512]{0:T(512)} %param.4) | copy-start | bytes 6148
  23.0 0.8 %copy-start = (bf16[1,64,512]{2,1,0:T(8,128)(2,1)S(1)}, bf16[1,64,512]{2,1,0:T(8,128)(2,1)}, u32[]{:S(2)}) copy-start(bf16[1,64,512]{2,1,0:T(8,128)(2,1)} %x_ref.3) | copy-start | bytes 196612

commit v2 on v1

--- a/solution.py
+++ b/solution.py
@@ -48,14 +48,12 @@
     return jnp.where(iota(x.shape, 1) < delay, 0.0, pltpu.roll(x, delay, 1))
 
 
-def moments_kernel(end_ref, x_ref, c_ref, e_ref):
-    x = x_ref[0].astype(F32)
+def moments(x, end):
     sensors, rows = x.shape
-    end = end_ref[0, 0]
     stack = [delayed(x, d) for d in range(LAGS + 1)] + [jnp.zeros_like(x)]
     z = jnp.concatenate(stack, axis=0).astype(BF16)
     xm = jnp.where(iota(x.shape, 1) < end, x, 0.0).astype(BF16)
-    c_ref[...] = dot_nt(xm, z).reshape(c_ref.shape)
+    c = dot_nt(xm, z)
     row, time = iota((16, rows), 0), iota((16, rows), 1)
     head_tail = jnp.where(row < 8, row, rows - 16 + row)
     last_live = jnp.where(row < 8, -1, end - 16 + row)
@@ -63,11 +61,11 @@
     sel_b = jnp.where(time == last_live, 1.0, 0.0).astype(BF16)
     xl = jnp.concatenate([x, jnp.zeros_like(x)], axis=0).astype(BF16)
     xr = jnp.concatenate([jnp.zeros_like(x), x], axis=0).astype(BF16)
-    e_ref[...] = (dot_nt(sel_a, xl) + dot_nt(sel_b, xr)).astype(BF16)
-
-
-def share_kernel(nblk, ngrp, ns, c_ref, e_ref, sum_ref, edge_ref,
-                 part, group_edge, prior, all_edge, mine, whole,
+    return c, (dot_nt(sel_a, xl) + dot_nt(sel_b, xr)).astype(BF16)
+
+
+def share_kernel(nblk, ngrp, ns, end_ref, x_ref, lag_ref, sum_ref, edge_ref, x_out, lagc_ref, lagr_ref,
+                 c_ref, e_ref, part, group_edge, prior, all_edge, mine, whole,
                  send1, recv1, send1e, recv1e, send2, recv2, send2e, recv2e, send3, recv3):
     b, g = lax.axis_index("blk"), lax.axis_index("grp")
     owner = (lambda i: True) if ns == nblk else (lambda i: i < ns)
@@ -85,6 +83,9 @@
         pl.semaphore_signal(barrier, inc=1, device_id=(lax.rem(b + off, nblk), g), device_id_type=MESH)
     for off in range(1, ngrp):
         pl.semaphore_signal(barrier, inc=1, device_id=(b, lax.rem(g + off, ngrp)), device_id_type=MESH)
+    c, e = moments(x_ref[0].astype(F32), end_ref[0, 0])
+    c_ref[...] = c.reshape(c_ref.shape)
+    e_ref[...] = e
     pl.semaphore_wait(barrier, nblk - 1 + ngrp - 1)
 
     def slice_copy(to, frm, off):
@@ -103,6 +104,10 @@
         edge_copy(to, b, off).start()
     when(owner(b), lambda: part.__setitem__(b, c_ref[b]))
     group_edge[b] = e_ref[...]
+    x_out[...] = x_ref[0]
+    lag = lag_ref[...].astype(F32)
+    lagr_ref[...] = jnp.broadcast_to(lag, lagr_ref.shape)
+    lagc_ref[...] = jnp.broadcast_to(lag, (TILE, lag.shape[1])).T
     for off in range(1, nblk):
         frm = lax.rem(b + nblk - off, nblk)
         when(owner(b), lambda: slice_copy(b, frm, off).wait_recv())
@@ -173,7 +178,7 @@
             edges_copy(h, g).wait_send()
 
 
-def lower_inverse(block, out_ref, r0):
+def lower_inverse(block, out_ref):
     n = TILE // 8
     lane, sub = iota((8, TILE), 1), iota((8, TILE), 0)
     x = [block[8 * r : 8 * r + 8, :] for r in range(n)]
@@ -184,38 +189,64 @@
     def rep_row(v, i):
         return jnp.broadcast_to(v[i : i + 1, :], (8, TILE))
 
+    def inverse(p):
+        return pl.reciprocal(p, approx=True)
+
     for q in range(n):
         first = 8 * q
+        last = q == n - 1
         cols = [rep_lane(x[q], first + j) for j in range(8)]
         t = {(i, j): rep_row(cols[j], i) for j in range(8) for i in range(j, 8)}
         inside = (lane >= first) & (lane < first + 8)
         aug = jnp.where(inside, jnp.where(lane - first == sub, 1.0, 0.0), x[q])
         y = [rep_row(aug, i) for i in range(8)]
-        inv, l, scaled = [], {}, []
-        for j in range(8):
-            p = t[j, j]
-            inv.append(1.0 / p)
-            scaled.append(y[j] * lax.rsqrt(p))
+        inv, l, scaled = [None] * 8, {}, [None] * 8
+        if not last:
+            m = [rep_lane(x[q + 1], first + j) for j in range(8)]
+            following = jnp.where(inside, 0.0, x[q + 1])
+        for j in range(0, 8, 2):
+            a, b, c = t[j, j], t[j + 1, j], t[j + 1, j + 1]
+            det = a * c - b * b
+            ia, idet = inverse(a), inverse(det)
+            ic = a * idet
+            inv[j], inv[j + 1] = ia, ic
+            rest = range(j + 2, 8)
             for i in range(j + 1, 8):
-                l[i, j] = t[i, j] * inv[j]
-            for k in range(j + 1, 8):
+                l[i, j] = t[i, j] * ia
+            e = {i: t[i, j + 1] - l[i, j] * b for i in rest}
+            for k in rest:
                 for i in range(k, 8):
-                    t[i, k] = t[i, k] - l[i, j] * t[k, j]
-            for i in range(j + 1, 8):
-                y[i] = y[i] - l[i, j] * y[j]
+                    t[i, k] = (t[i, k] - l[i, j] * t[k, j]) - (e[i] * e[k]) * ic
+            for i in rest:
+                l[i, j + 1] = e[i] * ic
+            y[j + 1] = y[j + 1] - l[j + 1, j] * y[j]
+            for i in rest:
+                y[i] = (y[i] - l[i, j] * y[j]) - l[i, j + 1] * y[j + 1]
+            if not last:
+                la = m[j] * ia
+                em = m[j + 1] - la * b
+                lc = em * ic
+                for k in rest:
+                    m[k] = (m[k] - la * t[k, j]) - lc * e[k]
+                following = (following - la * y[j]) - lc * y[j + 1]
+            scaled[j] = y[j] * lax.rsqrt(a)
+            scaled[j + 1] = y[j + 1] * lax.rsqrt(det * ia)
         rows = scaled[0]
         for i in range(1, 8):
             rows = jnp.where(sub == i, scaled[i], rows)
-        out_ref[pl.ds(pl.multiple_of(r0 + first, 8), 8), :] = jnp.where(lane < first + 8, rows, 0.0)
-        if q == n - 1:
+        out_ref[first : first + 8, :] = jnp.where(lane < first + 8, rows, 0.0)
+        if last:
             break
+        x[q + 1] = following
+        if q + 2 == n:
+            continue
         gs = [None] * 8
         for i in range(7, -1, -1):
             acc = y[i] * inv[i]
             for k in range(7, i, -1):
                 acc = acc - l[k, i] * gs[k]
             gs[i] = acc
-        for r in range(q + 1, n):
+        for r in range(q + 2, n):
             new = jnp.where(inside, 0.0, x[r])
             for j in range(7, -1, -1):
                 new = new - rep_lane(x[r], first + j) * gs[j]
@@ -223,10 +254,10 @@
 
 
 def fit_kernel(nblk, ngrp, x_ref, lagc_ref, lagr_ref, c_ref, e_ref, fac_ref, coef_ref, res_ref,
-               a, ps, pe, tl, vt, dm, miss, u, li, w):
+               a, ps, pe, tl, vt, dm, miss, u, li, w, v, d, row, li_now):
     b, g = lax.axis_index("blk"), lax.axis_index("grp")
     cols = a.shape[0]
-    x = x_ref[0].astype(F32)
+    x = x_ref[...].astype(F32)
     sensors, rows = x.shape
     half = nblk * 8
 
@@ -254,9 +285,9 @@
             for ref, at in ((ps, 0), (pe, half)):
                 part = jnp.where(left, ref[:, pl.ds(8 - even, 8), :], ref[:, pl.ds(8 - odd, 8), :])
                 vt[at : at + half, i * TILE : (i + 1) * TILE] = part.reshape(half, TILE)
-        v = vt[...]
-        signed = jnp.where(iota(v.shape, 0) < half, v, -v)
-        v16 = v.astype(BF16)
+        edges = vt[...]
+        signed = jnp.where(iota(edges.shape, 0) < half, edges, -edges)
+        v16 = edges.astype(BF16)
         dm[...] += dot(signed.T.astype(BF16), v16)
         miss[...] += dot(head.T.astype(BF16), v16[:half])
         return carry
@@ -277,8 +308,10 @@
     gram = gu + gu.T + dm[...] + eye
     cross = jnp.concatenate([c, jnp.zeros_like(c)], axis=0).T[sensors : sensors + cols, :]
     both = jnp.concatenate([gram, cross], axis=1)
-    pick = jnp.where(lagc_ref[...] == iota((cols, cols), 1), 1.0, 0.0).astype(BF16)
-    pick_t = jnp.where(lagr_ref[...] == iota((cols, cols), 0), 1.0, 0.0).astype(BF16)
+    lagc = jnp.concatenate([lagc_ref[...]] * (cols // TILE), axis=1).astype(jnp.int32)
+    lagr = lagr_ref[0:1, :].astype(jnp.int32)
+    pick = jnp.where(lagc == iota((cols, cols), 1), 1.0, 0.0).astype(BF16)
+    pick_t = jnp.where(lagr == iota((cols, cols), 0), 1.0, 0.0).astype(BF16)
     hi, mid, low = split3(both)
     turned = dot(pick, hi) + dot(pick, mid) + dot(pick, low)
     a[:, cols:] = turned[:, cols:]
@@ -286,29 +319,37 @@
     a[:, :cols] = dot(hi, pick_t) + dot(mid, pick_t) + dot(low, pick_t)
 
     steps = cols // TILE
+    u[...] = jnp.zeros_like(u)
+    d[...] = a[0:TILE, 0:TILE]
+    li[...] = jnp.zeros_like(li)
 
     def eliminate(k, carry):
         r0 = pl.multiple_of(k * TILE, TILE)
-        lower_inverse(a[pl.ds(r0, TILE), pl.ds(r0, TILE)], li, r0)
-        panel = exact_dot(li[pl.ds(r0, TILE), :], a[pl.ds(r0, TILE), :])
+        before = pl.multiple_of(jnp.maximum(k - 1, 0) * TILE, TILE)
+        row[...] = a[pl.ds(r0, TILE), :] - exact_dot(u[:, pl.ds(r0, TILE)].T, u[...])
+        v[pl.ds(before, TILE), :] = exact_dot(li[pl.ds(before, TILE), :].T, u[pl.ds(before, TILE), :])
+        lower_inverse(d[...], li_now)
+        now = li_now[...]
+        li[pl.ds(r0, TILE), :] = now
+        panel = exact_dot(now, row[...])
         panel = jnp.where(iota(panel.shape, 1) >= iota(panel.shape, 0) + r0, panel, 0.0)
         u[pl.ds(r0, TILE), :] = panel
 
         @pl.when(k < steps - 1)
         def _():
-            a[...] -= exact_dot(panel[:, :cols].T, panel)
+            r1 = pl.multiple_of(r0 + TILE, TILE)
+            above = u[:, pl.ds(r1, TILE)]
+            d[...] = a[pl.ds(r1, TILE), pl.ds(r1, TILE)] - exact_dot(above.T, above)
 
         return carry
 
     lax.fori_loop(0, steps, eliminate, 0)
 
-    w[...] = jnp.zeros_like(w)
-    for k in range(steps - 1, -1, -1):
-        at = slice(k * TILE, (k + 1) * TILE)
-        rhs = u[at, cols:]
-        if k < steps - 1:
-            rhs = rhs - exact_dot(u[at, (k + 1) * TILE : cols], w[(k + 1) * TILE :, :])
-        w[at, :] = exact_dot(li[at, :].T, rhs)
+    end = cols - TILE
+    w[end:, :] = exact_dot(li[end:, :].T, u[end:, cols:])
+    for k in range(steps - 2, -1, -1):
+        at, below = slice(k * TILE, (k + 1) * TILE), (k + 1) * TILE
+        w[at, :] = v[at, cols:] - exact_dot(v[at, below:cols], w[below:, :])
 
     share = cols // nblk
     row0 = pl.multiple_of(b * share, share)
@@ -336,19 +377,17 @@
     vmem = pl.BlockSpec(memory_space=VMEM)
     smem = pl.BlockSpec(memory_space=pltpu.SMEM)
     dma = pltpu.SemaphoreType.DMA
-    c, e = pl.pallas_call(
-        moments_kernel,
-        out_shape=(jax.ShapeDtypeStruct((ns, per, WIDE), F32), jax.ShapeDtypeStruct((16, TILE), BF16)),
-        in_specs=[smem, vmem],
-        out_specs=(vmem, vmem),
-    )(window_end, signal)
-    sums, edges = pl.pallas_call(
+    sums, edges, x, lagc, lagr = pl.pallas_call(
         functools.partial(share_kernel, nblk, ngrp, ns),
         out_shape=(jax.ShapeDtypeStruct((ns, per, WIDE), F32),
-                   jax.ShapeDtypeStruct((ngrp, nblk, 16, TILE), BF16)),
-        in_specs=[vmem, vmem],
-        out_specs=(vmem, vmem),
+                   jax.ShapeDtypeStruct((ngrp, nblk, 16, TILE), BF16),
+                   jax.ShapeDtypeStruct((sensors, rows), BF16),
+                   jax.ShapeDtypeStruct((cols, TILE), F32),
+                   jax.ShapeDtypeStruct((8, cols), F32)),
+        in_specs=[smem, vmem, vmem],
+        out_specs=(vmem,) * 5,
         scratch_shapes=[
+            VMEM((ns, per, WIDE), F32), VMEM((16, TILE), BF16),
             VMEM((nblk, per, WIDE), F32), VMEM((nblk, 16, TILE), BF16),
             VMEM((ngrp, per, WIDE), F32), VMEM((ngrp, nblk, 16, TILE), BF16),
             VMEM((per, WIDE), F32), VMEM((ns, per, WIDE), F32),
@@ -358,7 +397,7 @@
         ],
         compiler_params=pltpu.CompilerParams(
             collective_id=0, has_side_effects=True, vmem_limit_bytes=32 * 1024 * 1024),
-    )(c, e)
+    )(window_end, signal, lag_table.reshape(1, cols))
     half = nblk * 8
     share = cols // nblk
     return pl.pallas_call(
@@ -372,10 +411,11 @@
             VMEM((cols, WIDE), F32), VMEM((nblk, 16, TILE), F32), VMEM((nblk, 16, TILE), F32),
             VMEM((8, TILE), F32), VMEM((2 * half, cols), F32), VMEM((cols, cols), F32),
             VMEM((TILE, cols), F32), VMEM((cols, WIDE), F32), VMEM((cols, TILE), F32),
-            VMEM((cols, TILE), F32),
+            VMEM((cols, TILE), F32), VMEM((cols, WIDE), F32), VMEM((TILE, TILE), F32),
+            VMEM((TILE, WIDE), F32), VMEM((TILE, TILE), F32),
         ],
         compiler_params=pltpu.CompilerParams(vmem_limit_bytes=48 * 1024 * 1024),
-    )(signal, lag_table.reshape(cols, 1), lag_table.reshape(1, cols), sums, edges)
+    )(x, lagc, lagr, sums, edges)
 
 
 def solution(mesh):

time: 58.4 us -> 49.8 us (0.85)
  Pallas kernels: 53.1 us -> 46.8 us
  local copies, waits for them, and re-layouts: 3.11 us -> 0.85 us
    pallas_call x1, Pallas kernels: 33.7 us -> 29.4 us  [on_device(): pl.pallas_call(functools.partial(fit_kernel, nblk, ngrp), out_shape=(jax....]
    unnamed x8 -> x4, local copies, waits for them, and re-layouts: 2.97 us -> 0.85 us
    pallas_call x1 -> x0, Pallas kernels: 1.92 us -> none  [on_device(): pl.pallas_call(moments_kernel, out_shape=(jax.ShapeDtypeStruct((ns, per,...]
where the time goes in v2:
time: 49.8 us; the launch traced here: 49 us
  Pallas kernels  46.8 us (94%)
  between operations  1.31 us (3%)
  local copies, waits for them, and re-layouts  0.85 us (2%)
    pallas_call x1, Pallas kernels, on_device(): pl.pallas_call(functools.partial(fit_kernel, nblk, ngrp), out_shape=(jax....  29.4 us
    pallas_call x1, Pallas kernels, on_device(): pl.pallas_call(functools.partial(share_kernel, nblk, ngrp, ns), out_shape...  17.5 us

profile of v2, /device:TPU:5, one launch (start us, length us, event | category | flops | bytes accessed | tf_op | source)
XLA Modules:
  0.0 49.0 jit_solution(4267260436302745885)
XLA Ops:
  0.6 0.0 copy-start.1
  1.3 0.0 copy-done.1
  1.3 0.0 copy-start
  1.3 0.8 %copy-done = bf16[1,64,512]{2,1,0:T(8,128)(2,1)S(1)} copy-done((bf16[1,64,512]{2,1,0:T(8,128)(2,1)S(1)}, bf16[1,64,512]{2,1,0:T(8,128)(2,1)}, u32[]{:S(2)}) %copy-start) | copy-done | bytes 65560
  2.2 17.5 %shard_map.58 = (f32[8,8,640]{2,1,0:T(8,128)S(1)}, bf16[4,8,16,128]{3,2,1,0:T(8,128)(2,1)S(1)}, bf16[64,512]{1,0:T(8,128)(2,1)S(1)}, f32[512,128]{1,0:T(8,128)S(1)}, f32[8,512]{1,0:T(8,128)S(1)}) custom-call(s32[1,1]{1,0:T(1,128)S(6)} %copy.6.end_ref, bf16[1,64,512]{2,1,0:T(8,128)(2,1)S(1)} %copy-done, s32[1,512]{1,0:T(1,128)S(1)} %bitcast.1), custom_call_target="tpu_custom_call" | custom-call | tf_op jit(solution)/shard_map/pallas_call | solution.py:380
  19.6 29.4 %shard_map.59 = (f32[1,64,512]{2,1,0:T(8,128)}, f32[1,64,64]{2,1,0:T(8,128)}, f32[1,64,512]{2,1,0:T(8,128)}) custom-call(bf16[64,512]{1,0:T(8,128)(2,1)S(1)} %get-tuple-element.8.x_ref, f32[512,128]{1,0:T(8,128)S(1)} %get-tuple-element.9.lagc_ref, f32[8,512]{1,0:T(8,128)S(1)} %get-tuple-element.10.lagr_ref, f32[8,8,640]{2,1,0:T(8,128)S(1)} %get-tuple-element.11.c_ref, ...), custom_call_target="tpu_custom_call" | custom-call | tf_op jit(solution)/shard_map/pallas_call | solution.py:403
Async XLA Ops:
  0.6 0.7 %copy-start.1 = (s32[512]{0:T(512)S(1)}, s32[512]{0:T(512)}, u32[]{:S(2)}) copy-start(s32[512]{0:T(512)} %param.4) | copy-start | bytes 6148
  1.3 0.8 %copy-start = (bf16[1,64,512]{2,1,0:T(8,128)(2,1)S(1)}, bf16[1,64,512]{2,1,0:T(8,128)(2,1)}, u32[]{:S(2)}) copy-start(bf16[1,64,512]{2,1,0:T(8,128)(2,1)} %x_ref.1) | copy-start | bytes 196612

commit v3 on v2

v3 whole, which is shorter than its diff:
```python
import functools
import math

import jax
import jax.numpy as jnp
from jax import lax
from jax.experimental import pallas as pl
from jax.experimental.pallas import tpu as pltpu
from jax.sharding import PartitionSpec as P

ridge_weight = 4.0
LAGS = 8
TILE = 128
WIDE = 640
MESH = pl.DeviceIdType.MESH
VMEM = pltpu.VMEM
F32 = jnp.float32
BF16 = jnp.bfloat16


def iota(shape, dim):
    return lax.broadcasted_iota(jnp.int32, shape, dim)


def dot(a, b):
    return jnp.dot(a, b, preferred_element_type=F32)


def dot_nt(a, b):
    return lax.dot_general(a, b, (((1,), (1,)), ((), ())), preferred_element_type=F32)


def exact_dot(a, b):
    return jnp.dot(a, b, precision=lax.Precision.HIGHEST, preferred_element_type=F32)


def split3(x):
    hi = x.astype(BF16)
    rest = x - hi.astype(F32)
    mid = rest.astype(BF16)
    low = (rest - mid.astype(F32)).astype(BF16)
    return hi, mid, low


def delayed(x, delay):
    if delay == 0:
        return x
    return jnp.where(iota(x.shape, 1) < delay, 0.0, pltpu.roll(x, delay, 1))


def moments(x, end):
    sensors, rows = x.shape
    stack = [delayed(x, d) for d in range(LAGS + 1)] + [jnp.zeros_like(x)]
    z = jnp.concatenate(stack, axis=0).astype(BF16)
    xm = jnp.where(iota(x.shape, 1) < end, x, 0.0).astype(BF16)
    c = dot_nt(xm, z)
    row, time = iota((16, rows), 0), iota((16, rows), 1)
    head_tail = jnp.where(row < 8, row, rows - 16 + row)
    last_live = jnp.where(row < 8, -1, end - 16 + row)
    sel_a = jnp.where(time == head_tail, 1.0, 0.0).astype(BF16)
    sel_b = jnp.where(time == last_live, 1.0, 0.0).astype(BF16)
    xl = jnp.concatenate([x, jnp.zeros_like(x)], axis=0).astype(BF16)
    xr = jnp.concatenate([jnp.zeros_like(x), x], axis=0).astype(BF16)
    lagged = z[sensors : sensors * (LAGS + 1), :]
    return lagged, c, (dot_nt(sel_a, xl) + dot_nt(sel_b, xr)).astype(BF16)


def share_kernel(nblk, ngrp, ns, end_ref, x_ref, lag_ref,
                 sum_ref, x_out, pick_ref, pick_t_ref, zp_ref, dm, miss,
                 c_ref, e_ref, pair, acc, part, cls_edge, prior, all_edge, other_edge, mine, whole,
                 ps, pe, tl, vt,
                 send0, recv0, send1, recv1, send1e, recv1e, send2, recv2, send2e, recv2e,
                 send_pe, recv_pe, send3, send3p, recv3):
    b, g = lax.axis_index("blk"), lax.axis_index("grp")
    nz, nso, per = nblk // 2, ns // 2, part.shape[1]
    z, c = b // 2, lax.rem(b, 2)
    partner = 2 * z + 1 - c
    cols = dm.shape[0]
    half = nblk * 8
    owner = (lambda i: True) if nso == nz else (lambda i: i < nso)

    def when(cond, fn):
        if cond is True:
            fn()
        else:
            pl.when(cond)(fn)

    def remote(src, dst, send, recv, blk, grp):
        return pltpu.make_async_remote_copy(
            src_ref=src, dst_ref=dst, send_sem=send, recv_sem=recv,
            device_id=(blk, grp), device_id_type=MESH)

    def ahead(off):
        return lax.rem(z + off, nz)

    def behind(off):
        return lax.rem(z + nz - off, nz)

    prior[...] = jnp.zeros_like(prior)
    all_edge[...] = jnp.zeros_like(all_edge)
    barrier = pltpu.get_barrier_semaphore()
    pl.semaphore_signal(barrier, inc=1, device_id=(partner, g), device_id_type=MESH)
    for off in range(1, nz):
        pl.semaphore_signal(barrier, inc=1, device_id=(2 * ahead(off) + c, g), device_id_type=MESH)
    for off in range(1, ngrp):
        pl.semaphore_signal(barrier, inc=1, device_id=(b, lax.rem(g + off, ngrp)), device_id_type=MESH)
    x = x_ref[0].astype(F32)
    sensors = x.shape[0]
    lagged, moment, e = moments(x, end_ref[0, 0])
    for s in range(ns):
        c_ref[s % 2, s // 2] = moment[s * per : (s + 1) * per, :]
    e_ref[...] = e
    pl.semaphore_wait(barrier, nz + ngrp - 1)

    swap = remote(c_ref.at[1 - c], pair, send0, recv0, partner, g)
    swap.start()

    def edge_copy(to, frm, off):
        return remote(e_ref, cls_edge.at[frm], send1e.at[off], recv1e.at[frm], 2 * to + c, g)

    def slice_copy(to, frm, off):
        return remote(acc.at[to], part.at[frm], send1.at[off], recv1.at[frm], 2 * to + c, g)

    for off in range(1, nz):
        edge_copy(ahead(off), z, off).start()
    cls_edge[z] = e
    swap.wait_recv()
    acc[...] = c_ref[c] + pair[...]
    for off in range(1, nz):
        when(owner(ahead(off)), lambda: slice_copy(ahead(off), z, off).start())
    when(owner(z), lambda: part.__setitem__(z, acc[z]))

    x_out[...] = x_ref[0]
    lag = lag_ref[...]
    lag_col = jnp.broadcast_to(lag.astype(F32), (TILE, cols)).T.astype(jnp.int32)
    lag_col = jnp.concatenate([lag_col] * (cols // TILE), axis=1)
    pick = jnp.where(lag_col == iota((cols, cols), 1), 1.0, 0.0).astype(BF16)
    pick_t = jnp.where(lag == iota((cols, cols), 0), 1.0, 0.0).astype(BF16)
    pick_ref[...] = pick
    pick_t_ref[...] = pick_t
    zp_ref[...] = dot(pick, lagged).astype(BF16)

    for off in range(1, nz):
        when(owner(z), lambda: slice_copy(z, behind(off), off).wait_recv())
        edge_copy(z, behind(off), off).wait_recv()

    def total():
        out = part[0]
        for i in range(1, nz):
            out = out + part[i]
        mine[...] = out

    when(owner(z), total)
    all_edge[g] = cls_edge[...]

    def sum_copy(to, frm):
        return remote(mine, prior.at[frm], send2.at[to], recv2.at[frm], b, to)

    def edges_copy(to, frm):
        return remote(cls_edge, all_edge.at[frm], send2e.at[to], recv2e.at[frm], b, to)

    for h in range(1, ngrp):
        @pl.when(h > g)
        def _():
            when(owner(z), lambda: sum_copy(h, g).start())
            edges_copy(h, g).start()
    for h in range(ngrp - 1):
        @pl.when(h < g)
        def _():
            when(owner(z), lambda: sum_copy(g, h).wait_recv())

    def prefix():
        out = mine[...]
        for h in range(ngrp - 1):
            out = out + prior[h]
        whole[c, z] = out

    when(owner(z), prefix)

    def whole_copy(to, frm, off):
        return remote(whole.at[c, frm], whole.at[c, frm], send3.at[off], recv3.at[c, frm], 2 * to + c, g)

    def pair_copy(cls, frm):
        return remote(whole.at[cls, frm], whole.at[cls, frm], send3p.at[frm], recv3.at[cls, frm], partner, g)

    for off in range(1, nz):
        when(owner(z), lambda: whole_copy(ahead(off), z, off).start())
    when(owner(z), lambda: pair_copy(c, z).start())
    for h in range(ngrp - 1):
        @pl.when(h < g)
        def _():
            edges_copy(g, h).wait_recv()
    swap_edges = remote(all_edge, other_edge, send_pe, recv_pe, partner, g)
    swap_edges.start()
    ps[...] = jnp.zeros_like(ps)
    pe[...] = jnp.zeros_like(pe)
    tl[...] = jnp.zeros_like(tl)
    dm[...] = jnp.zeros_like(dm)
    miss[...] = jnp.zeros_like(miss)
    lane3 = iota((nblk, 16, TILE), 2)
    left = iota((nblk, 8, TILE), 2) < sensors
    swap_edges.wait_recv()

    def group_edges(h, carry):
        ours, theirs = all_edge[h].astype(F32), other_edge[h].astype(F32)
        first = jnp.where(c == 0, ours, theirs)
        second = jnp.where(c == 0, theirs, ours)
        e = jnp.stack([first, second], axis=1).reshape(nblk, 16, TILE)
        turned = pltpu.roll(e.reshape(nblk * 16, TILE), sensors, 1).reshape(nblk, 16, TILE)
        lo = jnp.where(lane3 < sensors, e, turned)
        hi = jnp.where(lane3 < sensors, turned, e)
        ps[0, 0:8, :] = tl[...]
        ps[1:, 0:8, :] = lo[: nblk - 1, 8:16, :]
        tl[...] = lo[nblk - 1, 8:16, :]
        pe[:, 0:8, :] = hi[:, 8:16, :]
        head = lo[:, 0:8, :].reshape(half, TILE)
        for i in range(LAGS // 2):
            even, odd = 2 * i + 1, 2 * i + 2
            for ref, at in ((ps, 0), (pe, half)):
                piece = jnp.where(left, ref[:, pl.ds(8 - even, 8), :], ref[:, pl.ds(8 - odd, 8), :])
                vt[at : at + half, i * TILE : (i + 1) * TILE] = piece.reshape(half, TILE)
        edges = vt[...].astype(BF16)
        turned_edges = dot(edges, pick_t_ref[...])
        signed = jnp.where(iota(turned_edges.shape, 0) < half, turned_edges, -turned_edges)
        dm[...] += dot(signed.T.astype(BF16), turned_edges.astype(BF16))
        miss[...] += dot(head.T.astype(BF16), edges[:half])[:sensors, :]
        return carry

    lax.fori_loop(0, g + 1, group_edges, 0)
    own = vt[pl.ds(pl.multiple_of(b * 8, 8), 8), :]
    own = jnp.concatenate([own, jnp.zeros((TILE - 8, cols), F32)], axis=0).astype(BF16)
    rim = dot(own, pick_t_ref[...]).T
    zp_ref[:, :TILE] = (zp_ref[:, :TILE].astype(F32) + rim).astype(BF16)

    for off in range(1, nz):
        frm = behind(off)

        def forward():
            whole_copy(z, frm, off).wait_recv()
            pair_copy(c, frm).start()

        when(owner(frm), forward)
    for i in range(nso):
        pair_copy(1 - c, i).wait_recv()
    for s in range(ns):
        sum_ref[s * per : (s + 1) * per, :] = whole[s % 2, s // 2]
    swap.wait_send()
    swap_edges.wait_send()
    for i in range(nso):
        pair_copy(c, i).wait_send()
    for off in range(1, nz):
        when(owner(ahead(off)), lambda: slice_copy(ahead(off), z, off).wait_send())
        edge_copy(ahead(off), z, off).wait_send()
        when(owner(z), lambda: whole_copy(ahead(off), z, off).wait_send())
    for h in range(1, ngrp):
        @pl.when(h > g)
        def _():
            when(owner(z), lambda: sum_copy(h, g).wait_send())
            edges_copy(h, g).wait_send()


def lower_inverse(block, out_ref):
    n = TILE // 8
    lane, sub = iota((8, TILE), 1), iota((8, TILE), 0)
    x = [block[8 * r : 8 * r + 8, :] for r in range(n)]

    def rep_lane(v, j):
        return jnp.broadcast_to(v[:, j : j + 1], (8, TILE))

    def rep_row(v, i):
        return jnp.broadcast_to(v[i : i + 1, :], (8, TILE))

    def inverse(p):
        return pl.reciprocal(p, approx=True)

    for q in range(n):
        first = 8 * q
        last = q == n - 1
        cols = [rep_lane(x[q], first + j) for j in range(8)]
        t = {(i, j): rep_row(cols[j], i) for j in range(8) for i in range(j, 8)}
        inside = (lane >= first) & (lane < first + 8)
        aug = jnp.where(inside, jnp.where(lane - first == sub, 1.0, 0.0), x[q])
        y = [rep_row(aug, i) for i in range(8)]
        inv, l, scaled = [None] * 8, {}, [None] * 8
        if not last:
            m = [rep_lane(x[q + 1], first + j) for j in range(8)]
            following = jnp.where(inside, 0.0, x[q + 1])
        for j in range(0, 8, 2):
            a, b, c = t[j, j], t[j + 1, j], t[j + 1, j + 1]
            det = a * c - b * b
            ia, idet = inverse(a), inverse(det)
            ic = a * idet
            inv[j], inv[j + 1] = ia, ic
            rest = range(j + 2, 8)
            for i in range(j + 1, 8):
                l[i, j] = t[i, j] * ia
            e = {i: t[i, j + 1] - l[i, j] * b for i in rest}
            for k in rest:
                for i in range(k, 8):
                    t[i, k] = (t[i, k] - l[i, j] * t[k, j]) - (e[i] * e[k]) * ic
            for i in rest:
                l[i, j + 1] = e[i] * ic
            y[j + 1] = y[j + 1] - l[j + 1, j] * y[j]
            for i in rest:
                y[i] = (y[i] - l[i, j] * y[j]) - l[i, j + 1] * y[j + 1]
            if not last:
                la = m[j] * ia
                em = m[j + 1] - la * b
                lc = em * ic
                for k in rest:
                    m[k] = (m[k] - la * t[k, j]) - lc * e[k]
                following = (following - la * y[j]) - lc * y[j + 1]
            scaled[j] = y[j] * lax.rsqrt(a)
            scaled[j + 1] = y[j + 1] * lax.rsqrt(det * ia)
        rows = scaled[0]
        for i in range(1, 8):
            rows = jnp.where(sub == i, scaled[i], rows)
        out_ref[first : first + 8, :] = jnp.where(lane < first + 8, rows, 0.0)
        if last:
            break
        x[q + 1] = following
        if q + 2 == n:
            continue
        gs = [None] * 8
        for i in range(7, -1, -1):
            acc = y[i] * inv[i]
            for k in range(7, i, -1):
                acc = acc - l[k, i] * gs[k]
            gs[i] = acc
        for r in range(q + 2, n):
            new = jnp.where(inside, 0.0, x[r])
            for j in range(7, -1, -1):
                new = new - rep_lane(x[r], first + j) * gs[j]
            x[r] = new


def fit_kernel(nblk, x_ref, pick_ref, pick_t_ref, zp_ref, dm_ref, miss_ref, c_ref, fac_ref, coef_ref, res_ref,
               a, u, li, w, v, d, row, li_now):
    b, g = lax.axis_index("blk"), lax.axis_index("grp")
    cols = a.shape[0]
    sensors, rows = x_ref.shape
    more = jnp.concatenate([miss_ref[...], jnp.zeros((sensors, TILE), F32)], axis=1)
    c = c_ref[...] + pltpu.roll(more, sensors, 1)
    cm = jnp.where(iota(c.shape, 1) < sensors, 0.5 * c, c)
    cr = pltpu.roll(cm, sensors, 1)
    a[...] = jnp.zeros_like(a)
    for i in range(LAGS):
        base = sensors * (i - i % 2)
        a[sensors * i : sensors * (i + 1), base:cols] = (cr if i % 2 else cm)[:, : cols - base]
    gu = a[:, :cols]
    ridge = (ridge_weight * nblk) * (g + 1).astype(F32)
    eye = jnp.where(iota((cols, cols), 0) == iota((cols, cols), 1), ridge, 0.0)
    gram = gu + gu.T
    cross = jnp.concatenate([c, jnp.zeros_like(c)], axis=0).T[sensors : sensors + cols, :]
    both = jnp.concatenate([gram, cross], axis=1)
    pick, pick_t = pick_ref[...], pick_t_ref[...]
    hi, mid, low = split3(both)
    turned = dot(pick, hi) + dot(pick, mid) + dot(pick, low)
    a[:, cols:] = turned[:, cols:]
    hi, mid, low = split3(turned[:, :cols])
    a[:, :cols] = dot(hi, pick_t) + dot(mid, pick_t) + dot(low, pick_t) + (dm_ref[...] + eye)

    steps = cols // TILE
    u[...] = jnp.zeros_like(u)
    d[...] = a[0:TILE, 0:TILE]
    li[...] = jnp.zeros_like(li)

    def eliminate(k, carry):
        r0 = pl.multiple_of(k * TILE, TILE)
        before = pl.multiple_of(jnp.maximum(k - 1, 0) * TILE, TILE)
        row[...] = a[pl.ds(r0, TILE), :] - exact_dot(u[:, pl.ds(r0, TILE)].T, u[...])
        v[pl.ds(before, TILE), :] = exact_dot(li[pl.ds(before, TILE), :].T, u[pl.ds(before, TILE), :])
        lower_inverse(d[...], li_now)
        now = li_now[...]
        li[pl.ds(r0, TILE), :] = now
        panel = exact_dot(now, row[...])
        panel = jnp.where(iota(panel.shape, 1) >= iota(panel.shape, 0) + r0, panel, 0.0)
        u[pl.ds(r0, TILE), :] = panel

        @pl.when(k < steps - 1)
        def _():
            r1 = pl.multiple_of(r0 + TILE, TILE)
            above = u[:, pl.ds(r1, TILE)]
            d[...] = a[pl.ds(r1, TILE), pl.ds(r1, TILE)] - exact_dot(above.T, above)

        return carry

    lax.fori_loop(0, steps, eliminate, 0)

    end = cols - TILE
    w[end:, :] = exact_dot(li[end:, :].T, u[end:, cols:])
    for k in range(steps - 2, -1, -1):
        at, below = slice(k * TILE, (k + 1) * TILE), (k + 1) * TILE
        w[at, :] = v[at, cols:] - exact_dot(v[at, below:cols], w[below:, :])

    share = cols // nblk
    row0 = pl.multiple_of(b * share, share)
    fac_ref[0] = u[pl.ds(row0, share), :cols] * (1.0 / math.sqrt(rows * nblk))
    coef_ref[0] = w[pl.ds(row0, share), :][:, :sensors]

    hi, mid, low = split3(w[...].T[:sensors, :])
    zp = zp_ref[...]
    res_ref[0] = x_ref[...].astype(F32) - (dot(hi, zp) + dot(mid, zp) + dot(low, zp))


def on_device(nblk, ngrp, signal, lag_table, window_end):
    _, sensors, rows = signal.shape
    cols = lag_table.shape[0]
    ns = min(nblk, sensors // 8)
    per = sensors // ns
    vmem = pl.BlockSpec(memory_space=VMEM)
    smem = pl.BlockSpec(memory_space=pltpu.SMEM)
    dma = pltpu.SemaphoreType.DMA
    half = nblk * 8
    nz, nso = nblk // 2, ns // 2
    share = cols // nblk
    sums, x, pick, pick_t, zp, dm, miss = pl.pallas_call(
        functools.partial(share_kernel, nblk, ngrp, ns),
        out_shape=(jax.ShapeDtypeStruct((sensors, WIDE), F32),
                   jax.ShapeDtypeStruct((sensors, rows), BF16),
                   jax.ShapeDtypeStruct((cols, cols), BF16),
                   jax.ShapeDtypeStruct((cols, cols), BF16),
                   jax.ShapeDtypeStruct((cols, rows), BF16),
                   jax.ShapeDtypeStruct((cols, cols), F32),
                   jax.ShapeDtypeStruct((sensors, cols), F32)),
        in_specs=[smem, vmem, vmem],
        out_specs=(vmem,) * 7,
        scratch_shapes=[
            VMEM((2, nso, per, WIDE), F32), VMEM((16, TILE), BF16),
            VMEM((nso, per, WIDE), F32), VMEM((nso, per, WIDE), F32),
            VMEM((nz, per, WIDE), F32), VMEM((nz, 16, TILE), BF16),
            VMEM((ngrp, per, WIDE), F32), VMEM((ngrp, nz, 16, TILE), BF16),
            VMEM((ngrp, nz, 16, TILE), BF16),
            VMEM((per, WIDE), F32), VMEM((2, nso, per, WIDE), F32),
            VMEM((nblk, 16, TILE), F32), VMEM((nblk, 16, TILE), F32), VMEM((8, TILE), F32),
            VMEM((2 * half, cols), F32),
            dma, dma, dma((nz,)), dma((nz,)), dma((nz,)), dma((nz,)),
            dma((ngrp,)), dma((ngrp,)), dma((ngrp,)), dma((ngrp,)),
            dma, dma, dma((nz,)), dma((nso,)), dma((2, nso)),
        ],
        compiler_params=pltpu.CompilerParams(
            collective_id=0, has_side_effects=True, vmem_limit_bytes=32 * 1024 * 1024),
    )(window_end, signal, lag_table.reshape(1, cols))
    return pl.pallas_call(
        functools.partial(fit_kernel, nblk),
        out_shape=(jax.ShapeDtypeStruct((1, share, cols), F32),
                   jax.ShapeDtypeStruct((1, share, sensors), F32),
                   jax.ShapeDtypeStruct((1, sensors, rows), F32)),
        in_specs=[vmem] * 7,
        out_specs=(vmem, vmem, vmem),
        scratch_shapes=[
            VMEM((cols, WIDE), F32), VMEM((cols, WIDE), F32), VMEM((cols, TILE), F32),
            VMEM((cols, TILE), F32), VMEM((cols, WIDE), F32), VMEM((TILE, TILE), F32),
            VMEM((TILE, WIDE), F32), VMEM((TILE, TILE), F32),
        ],
        compiler_params=pltpu.CompilerParams(vmem_limit_bytes=40 * 1024 * 1024),
    )(x, pick, pick_t, zp, dm, miss, sums)


def solution(mesh):
    return jax.shard_map(
        functools.partial(on_device, mesh.shape["blk"], mesh.shape["grp"]),
        mesh=mesh,
        in_specs=(P("grp", None, "blk"), P(), P("grp", "blk")),
        out_specs=(P("grp", "blk", None), P("grp", "blk", None), P("grp", None, "blk")),
        check_vma=False,
    )
```

time: 49.8 us -> 46.6 us (0.936); the launches traced: 49 us -> 46.4 us
  Pallas kernels: 46.8 us -> 44.3 us
    pallas_call x1, Pallas kernels: 29.4 us -> 27 us  [on_device(): pl.pallas_call(functools.partial(fit_kernel, nblk), out_shape=(jax.ShapeD...]
where the time goes in v3:
time: 46.6 us; the launch traced here: 46.4 us
  Pallas kernels  44.3 us (95%)
  between operations  1.31 us (3%)
  local copies, waits for them, and re-layouts  0.85 us (2%)
    pallas_call x1, Pallas kernels, on_device(): pl.pallas_call(functools.partial(fit_kernel, nblk), out_shape=(jax.ShapeD...  27 us
    pallas_call x1, Pallas kernels, on_device(): pl.pallas_call(functools.partial(share_kernel, nblk, ngrp, ns), out_shape...  17.3 us

profile of v3, /device:TPU:5, one launch (start us, length us, event | category | flops | bytes accessed | tf_op | source)
XLA Modules:
  0.0 46.4 jit_solution(154796650837140959)
XLA Ops:
  0.6 0.0 copy-start.1
  1.3 0.0 copy-done.1
  1.3 0.0 copy-start
  1.3 0.8 %copy-done = bf16[1,64,512]{2,1,0:T(8,128)(2,1)S(1)} copy-done((bf16[1,64,512]{2,1,0:T(8,128)(2,1)S(1)}, bf16[1,64,512]{2,1,0:T(8,128)(2,1)}, u32[]{:S(2)}) %copy-start) | copy-done | bytes 65560
  2.2 17.3 %shard_map.58 = (f32[64,640]{1,0:T(8,128)S(1)}, bf16[64,512]{1,0:T(8,128)(2,1)S(1)}, bf16[512,512]{1,0:T(8,128)(2,1)S(1)}, bf16[512,512]{1,0:T(8,128)(2,1)S(1)},...) custom-call(s32[1,1]{1,0:T(1,128)S(6)} %copy.6.end_ref, ...), custom_call_target="tpu_custom_call" | custom-call | tf_op jit(solution)/shard_map/pallas_call | solution.py:417
  19.5 27.0 %shard_map.59 = (f32[1,64,512]{2,1,0:T(8,128)}, f32[1,64,64]{2,1,0:T(8,128)}, f32[1,64,512]{2,1,0:T(8,128)}) custom-call(bf16[64,512]{1,0:T(8,128)(2,1)S(1)} %get-tuple-element.10.x_ref, bf16[512,512]{1,0:T(8,128)(2,1)S(1)} %get-tuple-element.11.pick_ref, bf16[512,512]{1,0:T(8,128)(2,1)S(1)} %get-tuple-element.12.pick_t_ref, ...), custom_call_target="tpu_custom_call" | custom-call | tf_op jit(solution)/shard_map/pallas_call | solution.py:444
Async XLA Ops:
  0.6 0.7 %copy-start.1 = (s32[512]{0:T(512)S(1)}, s32[512]{0:T(512)}, u32[]{:S(2)}) copy-start(s32[512]{0:T(512)} %param.4) | copy-start | bytes 6148
  1.3 0.8 %copy-start = (bf16[1,64,512]{2,1,0:T(8,128)(2,1)S(1)}, bf16[1,64,512]{2,1,0:T(8,128)(2,1)}, u32[]{:S(2)}) copy-start(bf16[1,64,512]{2,1,0:T(8,128)(2,1)} %x_ref.1) | copy-start | bytes 196612

commit v4 on v3

--- a/solution.py
+++ b/solution.py
@@ -65,12 +65,12 @@
     return lagged, c, (dot_nt(sel_a, xl) + dot_nt(sel_b, xr)).astype(BF16)
 
 
-def share_kernel(nblk, ngrp, ns, end_ref, x_ref, lag_ref,
+def share_kernel(nblk, ngrp, ns, end_hbm, x_hbm, lag_hbm,
                  sum_ref, x_out, pick_ref, pick_t_ref, zp_ref, dm, miss,
                  c_ref, e_ref, pair, acc, part, cls_edge, prior, all_edge, other_edge, mine, whole,
                  ps, pe, tl, vt,
                  send0, recv0, send1, recv1, send1e, recv1e, send2, recv2, send2e, recv2e,
-                 send_pe, recv_pe, send3, send3p, recv3):
+                 send_pe, recv_pe, send3, send3p, recv3, end_ref, lag_ref, x_ref, fetch):
     b, g = lax.axis_index("blk"), lax.axis_index("grp")
     nz, nso, per = nblk // 2, ns // 2, part.shape[1]
     z, c = b // 2, lax.rem(b, 2)
@@ -96,6 +96,10 @@
     def behind(off):
         return lax.rem(z + nz - off, nz)
 
+    loads = [pltpu.make_async_copy(src, dst, fetch.at[i])
+             for i, (src, dst) in enumerate(((x_hbm, x_ref), (end_hbm, end_ref), (lag_hbm, lag_ref)))]
+    for load in loads:
+        load.start()
     prior[...] = jnp.zeros_like(prior)
     all_edge[...] = jnp.zeros_like(all_edge)
     barrier = pltpu.get_barrier_semaphore()
@@ -104,6 +108,8 @@
         pl.semaphore_signal(barrier, inc=1, device_id=(2 * ahead(off) + c, g), device_id_type=MESH)
     for off in range(1, ngrp):
         pl.semaphore_signal(barrier, inc=1, device_id=(b, lax.rem(g + off, ngrp)), device_id_type=MESH)
+    for load in loads:
+        load.wait()
     x = x_ref[0].astype(F32)
     sensors = x.shape[0]
     lagged, moment, e = moments(x, end_ref[0, 0])
@@ -335,7 +341,7 @@
 
 
 def fit_kernel(nblk, x_ref, pick_ref, pick_t_ref, zp_ref, dm_ref, miss_ref, c_ref, fac_ref, coef_ref, res_ref,
-               a, u, li, w, v, d, row, li_now):
+               a, u, li, w, v, d, row, li_now, parts, dn):
     b, g = lax.axis_index("blk"), lax.axis_index("grp")
     cols = a.shape[0]
     sensors, rows = x_ref.shape
@@ -349,40 +355,44 @@
         a[sensors * i : sensors * (i + 1), base:cols] = (cr if i % 2 else cm)[:, : cols - base]
     gu = a[:, :cols]
     ridge = (ridge_weight * nblk) * (g + 1).astype(F32)
-    eye = jnp.where(iota((cols, cols), 0) == iota((cols, cols), 1), ridge, 0.0)
     gram = gu + gu.T
     cross = jnp.concatenate([c, jnp.zeros_like(c)], axis=0).T[sensors : sensors + cols, :]
     both = jnp.concatenate([gram, cross], axis=1)
-    pick, pick_t = pick_ref[...], pick_t_ref[...]
-    hi, mid, low = split3(both)
-    turned = dot(pick, hi) + dot(pick, mid) + dot(pick, low)
-    a[:, cols:] = turned[:, cols:]
-    hi, mid, low = split3(turned[:, :cols])
-    a[:, :cols] = dot(hi, pick_t) + dot(mid, pick_t) + dot(low, pick_t) + (dm_ref[...] + eye)
+    for i, piece in enumerate(split3(both)):
+        parts[i] = piece
+
+    def assemble(r):
+        pick = pick_ref[pl.ds(r, TILE), :]
+        turned = dot(pick, parts[0]) + dot(pick, parts[1]) + dot(pick, parts[2])
+        hi, mid, low = split3(turned[:, :cols])
+        pick_t = pick_t_ref[...]
+        eye = jnp.where(iota((TILE, cols), 0) + r == iota((TILE, cols), 1), ridge, 0.0)
+        gram = dot(hi, pick_t) + dot(mid, pick_t) + dot(low, pick_t) + (dm_ref[pl.ds(r, TILE), :] + eye)
+        a[pl.ds(r, TILE), :] = jnp.concatenate([gram, turned[:, cols:]], axis=1)
 
     steps = cols // TILE
     u[...] = jnp.zeros_like(u)
+    li[...] = jnp.zeros_like(li)
+    assemble(0)
     d[...] = a[0:TILE, 0:TILE]
-    li[...] = jnp.zeros_like(li)
 
     def eliminate(k, carry):
         r0 = pl.multiple_of(k * TILE, TILE)
         before = pl.multiple_of(jnp.maximum(k - 1, 0) * TILE, TILE)
+        r1 = pl.multiple_of(jnp.minimum(k + 1, steps - 1) * TILE, TILE)
         row[...] = a[pl.ds(r0, TILE), :] - exact_dot(u[:, pl.ds(r0, TILE)].T, u[...])
         v[pl.ds(before, TILE), :] = exact_dot(li[pl.ds(before, TILE), :].T, u[pl.ds(before, TILE), :])
+        above = u[:, pl.ds(r1, TILE)]
+        dn[...] = exact_dot(above.T, above)
+        assemble(r1)
         lower_inverse(d[...], li_now)
         now = li_now[...]
         li[pl.ds(r0, TILE), :] = now
         panel = exact_dot(now, row[...])
         panel = jnp.where(iota(panel.shape, 1) >= iota(panel.shape, 0) + r0, panel, 0.0)
         u[pl.ds(r0, TILE), :] = panel
-
-        @pl.when(k < steps - 1)
-        def _():
-            r1 = pl.multiple_of(r0 + TILE, TILE)
-            above = u[:, pl.ds(r1, TILE)]
-            d[...] = a[pl.ds(r1, TILE), pl.ds(r1, TILE)] - exact_dot(above.T, above)
-
+        new = u[pl.ds(r0, TILE), pl.ds(r1, TILE)]
+        d[...] = (a[pl.ds(r1, TILE), pl.ds(r1, TILE)] - dn[...]) - exact_dot(new.T, new)
         return carry
 
     lax.fori_loop(0, steps, eliminate, 0)
@@ -409,7 +419,6 @@
     ns = min(nblk, sensors // 8)
     per = sensors // ns
     vmem = pl.BlockSpec(memory_space=VMEM)
-    smem = pl.BlockSpec(memory_space=pltpu.SMEM)
     dma = pltpu.SemaphoreType.DMA
     half = nblk * 8
     nz, nso = nblk // 2, ns // 2
@@ -423,7 +432,7 @@
                    jax.ShapeDtypeStruct((cols, rows), BF16),
                    jax.ShapeDtypeStruct((cols, cols), F32),
                    jax.ShapeDtypeStruct((sensors, cols), F32)),
-        in_specs=[smem, vmem, vmem],
+        in_specs=[pl.BlockSpec(memory_space=pltpu.HBM)] * 3,
         out_specs=(vmem,) * 7,
         scratch_shapes=[
             VMEM((2, nso, per, WIDE), F32), VMEM((16, TILE), BF16),
@@ -437,6 +446,7 @@
             dma, dma, dma((nz,)), dma((nz,)), dma((nz,)), dma((nz,)),
             dma((ngrp,)), dma((ngrp,)), dma((ngrp,)), dma((ngrp,)),
             dma, dma, dma((nz,)), dma((nso,)), dma((2, nso)),
+            pltpu.SMEM((1, 1), jnp.int32), VMEM((1, cols), jnp.int32), VMEM((1, sensors, rows), BF16), dma((3,)),
         ],
         compiler_params=pltpu.CompilerParams(
             collective_id=0, has_side_effects=True, vmem_limit_bytes=32 * 1024 * 1024),
@@ -451,7 +461,7 @@
         scratch_shapes=[
             VMEM((cols, WIDE), F32), VMEM((cols, WIDE), F32), VMEM((cols, TILE), F32),
             VMEM((cols, TILE), F32), VMEM((cols, WIDE), F32), VMEM((TILE, TILE), F32),
-            VMEM((TILE, WIDE), F32), VMEM((TILE, TILE), F32),
+            VMEM((TILE, WIDE), F32), VMEM((TILE, TILE), F32), VMEM((3, cols, WIDE), BF16), VMEM((TILE, TILE), F32),
         ],
         compiler_params=pltpu.CompilerParams(vmem_limit_bytes=40 * 1024 * 1024),
     )(x, pick, pick_t, zp, dm, miss, sums)

time: 46.6 us -> 45 us (0.966)
  Pallas kernels: 44.3 us -> 42.6 us
    pallas_call x1, Pallas kernels: 27 us -> 25.3 us  [on_device(): pl.pallas_call(functools.partial(fit_kernel, nblk), out_shape=(jax.ShapeD...]
where the time goes in v4:
time: 45 us; the launch traced here: 44.8 us
  Pallas kernels  42.6 us (95%)
  between operations  1.31 us (3%)
  local copies, waits for them, and re-layouts  0.85 us (2%)
    pallas_call x1, Pallas kernels, on_device(): pl.pallas_call(functools.partial(fit_kernel, nblk), out_shape=(jax.ShapeD...  25.3 us
    pallas_call x1, Pallas kernels, on_device(): pl.pallas_call(functools.partial(share_kernel, nblk, ngrp, ns), out_shape...  17.3 us

profile of v4, /device:TPU:5, one launch (start us, length us, event | category | flops | bytes accessed | tf_op | source)
XLA Modules:
  0.0 44.8 jit_solution(5734996740129624585)
XLA Ops:
  0.6 0.0 copy-start.1
  1.3 0.0 copy-done.1
  1.3 0.0 copy-start
  1.3 0.8 %copy-done = bf16[1,64,512]{2,1,0:T(8,128)(2,1)S(1)} copy-done((bf16[1,64,512]{2,1,0:T(8,128)(2,1)S(1)}, bf16[1,64,512]{2,1,0:T(8,128)(2,1)}, u32[]{:S(2)}) %copy-start) | copy-done | bytes 65560
  2.2 17.3 %shard_map.58 = (f32[64,640]{1,0:T(8,128)S(1)}, bf16[64,512]{1,0:T(8,128)(2,1)S(1)}, bf16[512,512]{1,0:T(8,128)(2,1)S(1)}, bf16[512,512]{1,0:T(8,128)(2,1)S(1)},...) custom-call(s32[1,1]{1,0:T(1,128)S(6)} %copy.6.end_hbm, ...), custom_call_target="tpu_custom_call" | custom-call | tf_op jit(solution)/shard_map/pallas_call | solution.py:426
  19.5 25.3 %shard_map.59 = (f32[1,64,512]{2,1,0:T(8,128)}, f32[1,64,64]{2,1,0:T(8,128)}, f32[1,64,512]{2,1,0:T(8,128)}) custom-call(bf16[64,512]{1,0:T(8,128)(2,1)S(1)} %get-tuple-element.10.x_ref, bf16[512,512]{1,0:T(8,128)(2,1)S(1)} %get-tuple-element.11.pick_ref, bf16[512,512]{1,0:T(8,128)(2,1)S(1)} %get-tuple-element.12.pick_t_ref, ...), custom_call_target="tpu_custom_call" | custom-call | tf_op jit(solution)/shard_map/pallas_call | solution.py:454
Async XLA Ops:
  0.6 0.7 %copy-start.1 = (s32[512]{0:T(512)S(1)}, s32[512]{0:T(512)}, u32[]{:S(2)}) copy-start(s32[512]{0:T(512)} %param.4) | copy-start | bytes 6148
  1.3 0.8 %copy-start = (bf16[1,64,512]{2,1,0:T(8,128)(2,1)S(1)}, bf16[1,64,512]{2,1,0:T(8,128)(2,1)}, u32[]{:S(2)}) copy-start(bf16[1,64,512]{2,1,0:T(8,128)(2,1)} %x_hbm.1) | copy-start | bytes 196612

commit v5 on v4

--- a/solution.py
+++ b/solution.py
@@ -376,26 +376,31 @@
     assemble(0)
     d[...] = a[0:TILE, 0:TILE]
 
+    row[...] = jnp.zeros_like(row)
+
+    def factor_rows(r):
+        panel = exact_dot(li[pl.ds(r, TILE), :], row[...])
+        u[pl.ds(r, TILE), :] = jnp.where(iota(panel.shape, 1) >= iota(panel.shape, 0) + r, panel, 0.0)
+
     def eliminate(k, carry):
         r0 = pl.multiple_of(k * TILE, TILE)
         before = pl.multiple_of(jnp.maximum(k - 1, 0) * TILE, TILE)
         r1 = pl.multiple_of(jnp.minimum(k + 1, steps - 1) * TILE, TILE)
+        factor_rows(before)
+        v[pl.ds(before, TILE), :] = exact_dot(li[pl.ds(before, TILE), :].T, u[pl.ds(before, TILE), :])
         row[...] = a[pl.ds(r0, TILE), :] - exact_dot(u[:, pl.ds(r0, TILE)].T, u[...])
-        v[pl.ds(before, TILE), :] = exact_dot(li[pl.ds(before, TILE), :].T, u[pl.ds(before, TILE), :])
         above = u[:, pl.ds(r1, TILE)]
         dn[...] = exact_dot(above.T, above)
         assemble(r1)
         lower_inverse(d[...], li_now)
         now = li_now[...]
         li[pl.ds(r0, TILE), :] = now
-        panel = exact_dot(now, row[...])
-        panel = jnp.where(iota(panel.shape, 1) >= iota(panel.shape, 0) + r0, panel, 0.0)
-        u[pl.ds(r0, TILE), :] = panel
-        new = u[pl.ds(r0, TILE), pl.ds(r1, TILE)]
+        new = exact_dot(now, row[:, pl.ds(r1, TILE)])
         d[...] = (a[pl.ds(r1, TILE), pl.ds(r1, TILE)] - dn[...]) - exact_dot(new.T, new)
         return carry
 
     lax.fori_loop(0, steps, eliminate, 0)
+    factor_rows(cols - TILE)
 
     end = cols - TILE
     w[end:, :] = exact_dot(li[end:, :].T, u[end:, cols:])

time: 45 us -> 44.7 us (level)
  no operation moved by 1% of the time
where the time goes in v5:
time: 44.7 us; the launch traced here: 44.6 us
  Pallas kernels  42.4 us (95%)
  between operations  1.31 us (3%)
  local copies, waits for them, and re-layouts  0.85 us (2%)
    pallas_call x1, Pallas kernels, on_device(): pl.pallas_call(functools.partial(fit_kernel, nblk), out_shape=(jax.ShapeD...  25.1 us
    pallas_call x1, Pallas kernels, on_device(): pl.pallas_call(functools.partial(share_kernel, nblk, ngrp, ns), out_shape...  17.3 us

profile of v5, /device:TPU:5, one launch (start us, length us, event | category | flops | bytes accessed | tf_op | source)
XLA Modules:
  0.0 44.6 jit_solution(8749537737185595823)
XLA Ops:
  0.6 0.0 copy-start.1
  1.3 0.0 copy-done.1
  1.3 0.0 copy-start
  1.3 0.8 %copy-done = bf16[1,64,512]{2,1,0:T(8,128)(2,1)S(1)} copy-done((bf16[1,64,512]{2,1,0:T(8,128)(2,1)S(1)}, bf16[1,64,512]{2,1,0:T(8,128)(2,1)}, u32[]{:S(2)}) %copy-start) | copy-done | bytes 65560
  2.2 17.3 %shard_map.58 = (f32[64,640]{1,0:T(8,128)S(1)}, bf16[64,512]{1,0:T(8,128)(2,1)S(1)}, bf16[512,512]{1,0:T(8,128)(2,1)S(1)}, bf16[512,512]{1,0:T(8,128)(2,1)S(1)},...) custom-call(s32[1,1]{1,0:T(1,128)S(6)} %copy.6.end_hbm, ...), custom_call_target="tpu_custom_call" | custom-call | tf_op jit(solution)/shard_map/pallas_call | solution.py:431
  19.5 25.1 %shard_map.59 = (f32[1,64,512]{2,1,0:T(8,128)}, f32[1,64,64]{2,1,0:T(8,128)}, f32[1,64,512]{2,1,0:T(8,128)}) custom-call(bf16[64,512]{1,0:T(8,128)(2,1)S(1)} %get-tuple-element.10.x_ref, bf16[512,512]{1,0:T(8,128)(2,1)S(1)} %get-tuple-element.11.pick_ref, bf16[512,512]{1,0:T(8,128)(2,1)S(1)} %get-tuple-element.12.pick_t_ref, ...), custom_call_target="tpu_custom_call" | custom-call | tf_op jit(solution)/shard_map/pallas_call | solution.py:459
Async XLA Ops:
  0.6 0.7 %copy-start.1 = (s32[512]{0:T(512)S(1)}, s32[512]{0:T(512)}, u32[]{:S(2)}) copy-start(s32[512]{0:T(512)} %param.4) | copy-start | bytes 6148
  1.3 0.8 %copy-start = (bf16[1,64,512]{2,1,0:T(8,128)(2,1)S(1)}, bf16[1,64,512]{2,1,0:T(8,128)(2,1)}, u32[]{:S(2)}) copy-start(bf16[1,64,512]{2,1,0:T(8,128)(2,1)} %x_hbm.1) | copy-start | bytes 196612

commit v6 on v5

--- a/solution.py
+++ b/solution.py
@@ -233,19 +233,19 @@
         return carry
 
     lax.fori_loop(0, g + 1, group_edges, 0)
+    for off in range(1, nz):
+        frm = behind(off)
+
+        def forward():
+            whole_copy(z, frm, off).wait_recv()
+            pair_copy(c, frm).start()
+
+        when(owner(frm), forward)
     own = vt[pl.ds(pl.multiple_of(b * 8, 8), 8), :]
     own = jnp.concatenate([own, jnp.zeros((TILE - 8, cols), F32)], axis=0).astype(BF16)
     rim = dot(own, pick_t_ref[...]).T
     zp_ref[:, :TILE] = (zp_ref[:, :TILE].astype(F32) + rim).astype(BF16)
 
-    for off in range(1, nz):
-        frm = behind(off)
-
-        def forward():
-            whole_copy(z, frm, off).wait_recv()
-            pair_copy(c, frm).start()
-
-        when(owner(frm), forward)
     for i in range(nso):
         pair_copy(1 - c, i).wait_recv()
     for s in range(ns):

time: 44.7 us -> 44.7 us (level)
  no operation moved by 1% of the time
where the time goes in v6:
time: 44.7 us; the launch traced here: 44.6 us
  Pallas kernels  42.4 us (95%)
  between operations  1.31 us (3%)
  local copies, waits for them, and re-layouts  0.85 us (2%)
    pallas_call x1, Pallas kernels, on_device(): pl.pallas_call(functools.partial(fit_kernel, nblk), out_shape=(jax.ShapeD...  25.1 us
    pallas_call x1, Pallas kernels, on_device(): pl.pallas_call(functools.partial(share_kernel, nblk, ngrp, ns), out_shape...  17.3 us

profile of v6, /device:TPU:5, one launch (start us, length us, event | category | flops | bytes accessed | tf_op | source)
XLA Modules:
  0.0 44.6 jit_solution(9971826396588901177)
XLA Ops:
  0.6 0.0 copy-start.1
  1.3 0.0 copy-done.1
  1.3 0.0 copy-start
  1.3 0.8 %copy-done = bf16[1,64,512]{2,1,0:T(8,128)(2,1)S(1)} copy-done((bf16[1,64,512]{2,1,0:T(8,128)(2,1)S(1)}, bf16[1,64,512]{2,1,0:T(8,128)(2,1)}, u32[]{:S(2)}) %copy-start) | copy-done | bytes 65560
  2.2 17.3 %shard_map.58 = (f32[64,640]{1,0:T(8,128)S(1)}, bf16[64,512]{1,0:T(8,128)(2,1)S(1)}, bf16[512,512]{1,0:T(8,128)(2,1)S(1)}, bf16[512,512]{1,0:T(8,128)(2,1)S(1)},...) custom-call(s32[1,1]{1,0:T(1,128)S(6)} %copy.6.end_hbm, ...), custom_call_target="tpu_custom_call" | custom-call | tf_op jit(solution)/shard_map/pallas_call | solution.py:431
  19.5 25.1 %shard_map.59 = (f32[1,64,512]{2,1,0:T(8,128)}, f32[1,64,64]{2,1,0:T(8,128)}, f32[1,64,512]{2,1,0:T(8,128)}) custom-call(bf16[64,512]{1,0:T(8,128)(2,1)S(1)} %get-tuple-element.10.x_ref, bf16[512,512]{1,0:T(8,128)(2,1)S(1)} %get-tuple-element.11.pick_ref, bf16[512,512]{1,0:T(8,128)(2,1)S(1)} %get-tuple-element.12.pick_t_ref, ...), custom_call_target="tpu_custom_call" | custom-call | tf_op jit(solution)/shard_map/pallas_call | solution.py:459
Async XLA Ops:
  0.6 0.7 %copy-start.1 = (s32[512]{0:T(512)S(1)}, s32[512]{0:T(512)}, u32[]{:S(2)}) copy-start(s32[512]{0:T(512)} %param.4) | copy-start | bytes 6148
  1.3 0.8 %copy-start = (bf16[1,64,512]{2,1,0:T(8,128)(2,1)S(1)}, bf16[1,64,512]{2,1,0:T(8,128)(2,1)}, u32[]{:S(2)}) copy-start(bf16[1,64,512]{2,1,0:T(8,128)(2,1)} %x_hbm.1) | copy-start | bytes 196612
